TPU v7x, 32 devices: a whole 2x2x4 slice. The times are simulated.
32 devices in a mesh: dp: 8 (over y, x, core), tensor: 4 (over z).
Axes of the slice: x: 2, y: 2, z: 4, core: 2. Of those that a mesh axis runs over, the one named last changes fastest.
Arguments:
- inputs: bfloat16 [8192, 8192], P('dp', 'tensor'), may hold values from -6 to 6
- frozen_value_weight: bfloat16 [8192, 1024], P('tensor'), may hold values from -0.0625 to 0.0625
- adapter_down_weight: bfloat16 [128, 8192, 64], P('dp', 'tensor'), may hold values from -0.0625 to 0.0625
- adapter_up_weight: bfloat16 [128, 64, 1024], P('dp', None, 'tensor'), may hold values from -0.75 to 0.75
- adapter_per_block: int32 [64], P('dp'), may hold values from 0 to 127, as said below
- adapter_storage_index: int32 [128], replicated, may hold values from 0 to 127, as said below
- value_gradient: bfloat16 [8192, 1024], P('dp', 'tensor'), may hold values from -6 to 6
Outputs:
- values: bfloat16 [8192, 1024], P('dp', 'tensor')
- grad_inputs: bfloat16 [8192, 8192], P('dp', 'tensor')
- grad_down: bfloat16 [128, 8192, 64], P('dp', 'tensor')
- grad_up: bfloat16 [128, 64, 1024], P('dp', None, 'tensor')
Inputs may be any that keep to these rules, and one draw needn't show every extreme that they name: Adapter a is kept by data device adapter_storage_index[a] // 16; adapter_storage_index is a permutation. `adapter_per_block`: the 8 blocks of one data device use adapters kept by pairwise different data devices; in every draw there is one data device whose adapters are used by a block of every data device, so that keeper serves all 8 data devices.
All inputs are finite; a program needn't handle non-finite values.
Results may differ from a plain program's by a relative error of at most 0.0054.
Values may be sent and summed in bfloat16 or wider, within the bound.
No kernel may reach another device: no remote copies, remote signals or barrier semaphores. Data moves between devices by JAX's collectives and lax.ppermute only.
A program may use at most 128 MiB of HBM per device.

v0:
```python
import jax
import jax.numpy as jnp
from jax import lax
from jax.sharding import PartitionSpec as P

BLOCK = 128


adapter_scale = 0.5


def on_device(
    inputs,
    frozen_value_weight,
    adapter_down_weight,
    adapter_up_weight,
    adapter_per_block,
    adapter_storage_index,
    value_gradient,
):
    count_dp = lax.axis_size("dp")
    nblocks = adapter_per_block.shape[0]
    retained_rows = adapter_down_weight.shape[0]
    rows_per_worker = inputs.shape[0]
    feat = inputs.shape[1]
    column_range = value_gradient.shape[1]
    spot = adapter_storage_index[adapter_per_block]
    keeper = spot // retained_rows
    owner_ids = jnp.arange(count_dp, dtype=jnp.int32)
    match = keeper[None, :] == owner_ids[:, None]
    wanted = jnp.sum(jnp.where(match, spot[None, :] % retained_rows + 1, 0), axis=1) - 1
    asked = lax.all_to_all(wanted[:, None], "dp", split_axis=0, concat_axis=0, tiled=True)
    selected_adapter = (asked == jnp.arange(retained_rows, dtype=jnp.int32)[None, :]).astype(
        jnp.bfloat16
    )
    reply_down = jnp.einsum(
        "ig,gnx->inx", selected_adapter, adapter_down_weight, preferred_element_type=jnp.float32
    ).astype(jnp.bfloat16)
    returned_up_matrix = jnp.einsum(
        "cf,fxj->cxj", selected_adapter, adapter_up_weight, preferred_element_type=jnp.float32
    ).astype(jnp.bfloat16)
    fetched_down, fetched_up = (
        lax.all_to_all(reply_down, "dp", split_axis=0, concat_axis=0, tiled=True),
        lax.all_to_all(returned_up_matrix, "dp", split_axis=0, concat_axis=0, tiled=True),
    )
    block_down = jnp.take(fetched_down, keeper, axis=0)
    block_up = jnp.take(fetched_up, keeper, axis=0)
    x_blocks = inputs.reshape(nblocks, BLOCK, feat)
    low_part = jnp.einsum("bnd,bdr->bnr", x_blocks, block_down, preferred_element_type=jnp.float32)
    partial_base = jnp.dot(inputs, frozen_value_weight, preferred_element_type=jnp.float32)
    low = lax.psum(low_part, "tensor").astype(jnp.bfloat16)
    frozen_output = lax.psum_scatter(partial_base, "tensor", scatter_dimension=1, tiled=True)
    raised_output = jnp.einsum("bnr,brk->bnk", low, block_up, preferred_element_type=jnp.float32)
    values = (
        frozen_output + adapter_scale * raised_output.reshape(rows_per_worker, column_range)
    ).astype(jnp.bfloat16)
    dy_blocks = value_gradient.reshape(nblocks, BLOCK, column_range)
    partial_low_gradient = adapter_scale * jnp.einsum(
        "bnk,brk->bnr", dy_blocks, block_up, preferred_element_type=jnp.float32
    )
    low_rank_gradient = lax.psum(partial_low_gradient, "tensor").astype(jnp.bfloat16)
    grad_base = lax.dot_general(
        lax.all_gather(value_gradient, "tensor", axis=1, tiled=True),
        frozen_value_weight,
        (((1,), (1,)), ((), ())),
        preferred_element_type=jnp.float32,
    )
    back = jnp.einsum(
        "bnr,bdr->bnd", low_rank_gradient, block_down, preferred_element_type=jnp.float32
    )
    grad_inputs = (grad_base + back.reshape(rows_per_worker, feat)).astype(jnp.bfloat16)
    route = match.astype(jnp.bfloat16)
    term_down = jnp.einsum(
        "bnd,bnr->bdr", x_blocks, low_rank_gradient, preferred_element_type=jnp.float32
    ).astype(jnp.bfloat16)
    term_up = jnp.einsum("bnr,bnk->brk", low, dy_blocks, preferred_element_type=jnp.float32).astype(
        jnp.bfloat16
    )
    send_down = jnp.einsum(
        "ob,bdr->odr", route, term_down, preferred_element_type=jnp.float32
    ).astype(jnp.bfloat16)
    send_up = jnp.einsum("ob,brk->ork", route, term_up, preferred_element_type=jnp.float32).astype(
        jnp.bfloat16
    )
    got_down, got_up = (
        lax.all_to_all(send_down, "dp", split_axis=0, concat_axis=0, tiled=True),
        lax.all_to_all(send_up, "dp", split_axis=0, concat_axis=0, tiled=True),
    )
    grad_down = jnp.einsum(
        "sa,sdr->adr", selected_adapter, got_down, preferred_element_type=jnp.float32
    ).astype(jnp.bfloat16)
    grad_up = jnp.einsum(
        "sa,srk->ark", selected_adapter, got_up, preferred_element_type=jnp.float32
    ).astype(jnp.bfloat16)
    return (values, grad_inputs, grad_down, grad_up)


def solution(mesh):
    return jax.shard_map(
        on_device,
        mesh=mesh,
        in_specs=(
            P("dp", "tensor"),
            P("tensor", None),
            P("dp", "tensor", None),
            P("dp", None, "tensor"),
            P("dp"),
            P(),
            P("dp", "tensor"),
        ),
        out_specs=(
            P("dp", "tensor"),
            P("dp", "tensor"),
            P("dp", "tensor", None),
            P("dp", None, "tensor"),
        ),
        check_vma=False,
    )
```

profile of v0, /device:TPU:0, one launch (start us, length us, event | category | flops | bytes accessed | tf_op | source)
XLA Modules:
  0.0 186.6 jit_solution(16865574206655064935)
XLA Ops:
  7.2 0.0 copy-start
  7.2 0.0 all-gather.2.cloned.1.call-start
  7.2 0.7 all-gather.2.cloned.1.call-update
  7.9 0.0 reduce-scatter.2.cloned.1.call-start
  8.0 9.9 %fusion.39 = f32[1024,1024]{1,0:T(8,128)} fusion(bf16[1024,2048]{1,0:T(8,128)(2,1)} %param.7, bf16[2048,1024]{1,0:T(8,128)(2,1)} %param.8), kind=kOutput, calls=%fused_computation.68 | convolution fusion | flops 4294967296 | bytes 12582912 | tf_op jit(solution)/shard_map/dot_general | solution.py:50
  17.9 0.0 copy-start.8
  17.9 0.0 copy-start.1
  17.9 0.0 reduce-scatter.2.cloned.1.call-update
  17.9 0.6 copy-done.8
  18.6 0.0 copy-done.1
  18.6 0.6 gather_fusion
  19.2 0.1 select_reduce_fusion
  19.4 0.1 copy.38
  19.4 9.6 %all_to_all.26 = s32[8,1,1]{2,1,0:T(1,128)S(1)} all-to-all(s32[8,1,1]{2,1,0:T(1,128)S(1)} %copy.38), channel_id=1, replica_groups=mesh['dp'=8,'tensor'=4] {'dp'}, dimensions={0} | all-to-all | bytes 64 | tf_op jit(solution)/shard_map/all_to_all | solution.py:32
  29.1 0.2 reduce
  29.3 0.0 copy-done
  29.3 0.4 convolution_convert_fusion.4
  29.7 0.8 copy.42
  30.5 3.4 %all-to-all-start.2 = ((bf16[8,64,256]{2,1,0:T(8,128)(2,1)}), bf16[8,64,256]{2,1,0:T(8,128)(2,1)S(1)}, u32[]{:S(2)}, u32[]{:S(2)}) async-start(bf16[8,64,256]{2,1,0:T(8,128)(2,1)} %copy.42), calls=%async_computation.3 | async-start | bytes 524288 | tf_op jit(solution)/shard_map/all_to_all | solution.py:44
  33.9 6.8 %fusion.3 = bf16[8,2048,64]{1,0,2:T(8,128)(2,1)S(1)} fusion(bf16[16,2048,64]{1,2,0:T(8,128)(2,1)} %param.9, s32[8]{0:T(128)S(1)} %reduce), kind=kOutput, calls=%fused_computation.8 | convolution fusion | flops 34603136 | bytes 6291488 | tf_op jit(solution)/shard_map/ig,gnx->inx/dot_general | solution.py:36
  40.7 0.0 copy-start.3
  40.7 2.5 %copy.40 = bf16[8,2048,64]{1,2,0:T(8,128)(2,1)} copy(bf16[8,2048,64]{1,0,2:T(8,128)(2,1)S(1)} %fusion.3) | data formatting | bytes 4194304 | tf_op jit(solution)/shard_map/convert_element_type | solution.py:38
  43.2 0.0 all-to-all-done.2
  43.2 0.0 copy-start.4
  43.2 0.7 copy-done.4
  43.9 4.1 %all-to-all-start.1 = ((bf16[8,2048,64]{1,2,0:T(8,128)(2,1)}), bf16[8,2048,64]{1,2,0:T(8,128)(2,1)S(1)}, u32[]{:S(2)}, u32[]{:S(2)}) async-start(bf16[8,2048,64]{1,2,0:T(8,128)(2,1)} %copy.40), calls=%async_computation.2 | async-start | bytes 4194304 | tf_op jit(solution)/shard_map/all_to_all | solution.py:43
  48.0 1.5 gather_fusion.2
  49.5 0.0 copy-done.3
  49.6 1.1 fusion.9
  50.6 24.0 %all-to-all-done.1 = bf16[8,2048,64]{1,2,0:T(8,128)(2,1)S(1)} async-done(((bf16[8,2048,64]{1,2,0:T(8,128)(2,1)}), bf16[8,2048,64]{1,2,0:T(8,128)(2,1)S(1)}, u32[]{:S(2)}, u32[]{:S(2)}) %all-to-all-start.1) | async-done | bytes 2097184 | tf_op jit(solution)/shard_map/all_to_all | solution.py:43
  74.6 2.0 %gather_fusion.1 = bf16[8,2048,64]{1,2,0:T(8,128)(2,1)} fusion(bf16[8,2048,64]{1,2,0:T(8,128)(2,1)S(1)} %all-to-all-done.1, s32[1024]{0:T(1024)S(1)} %pad_clamp_fusion), kind=kCustom, calls=%fused_computation.1 | custom fusion | bytes 4194336 | tf_op jit(solution)/shard_map/jit(_take)/gather | solution.py:46
  76.6 0.0 copy-start.5
  76.6 4.5 %convolution_bitcast_fusion = f32[8,128,64]{1,2,0:T(8,128)S(1)} fusion(bf16[8,128,2048]{2,1,0:T(8,128)(2,1)} %bitcast.54, bf16[8,2048,64]{1,2,0:T(8,128)(2,1)} %gather_fusion.1, pred[8]{0:T(512)(128)(4,1)S(1)} %get-tuple-element.22), kind=kOutput, calls=%fused_computation.22 | convolution fusion | flops 269484032 | bytes 6553608 | tf_op jit(solution)/shard_map/bnd,bdr->bnr/dot_general | solution.py:49
  81.1 0.0 copy-done.5
  81.1 46.2 %all-reduce.2 = (bf16[8,128,64]{1,2,0:T(8,128)(2,1)S(1)}, bf16[8,128,64]{1,2,0:T(8,128)(2,1)S(1)}) all-reduce(f32[8,128,64]{1,2,0:T(8,128)S(1)} %convolution_bitcast_fusion, f32[8,128,64]{1,2,0:T(8,128)S(1)} %copy-done.5), channel_id=1, replica_groups=mesh['dp'=8,'tensor'=4] {'tensor'}, use_global_device_ids=true, to_apply=%region_2.3 | all-reduce | flops 131072 | bytes 786432 | tf_op jit(solution)/shard_map/psum | solution.py:51
  127.4 0.0 copy-start.6
  127.4 0.2 convolution_convert_fusion.6
  127.6 0.2 convolution_convert_fusion.5
  127.9 0.8 copy.47
  128.6 3.4 %all-to-all-start.4 = ((bf16[8,64,256]{2,1,0:T(8,128)(2,1)}), bf16[8,64,256]{2,1,0:T(8,128)(2,1)S(1)}, u32[]{:S(2)}, u32[]{:S(2)}) async-start(bf16[8,64,256]{2,1,0:T(8,128)(2,1)} %copy.47), calls=%async_computation.5 | async-start | bytes 524288 | tf_op jit(solution)/shard_map/all_to_all | solution.py:87
  132.0 2.9 %fusion.6 = bf16[8,2048,64]{1,2,0:T(8,128)(2,1)S(1)} fusion(bf16[8,128,2048]{2,1,0:T(8,128)(2,1)} %bitcast.55, bf16[8,128,64]{1,2,0:T(8,128)(2,1)S(1)} %get-tuple-element.21), kind=kOutput, calls=%fused_computation.11 | convolution fusion | flops 269484032 | bytes 6422528 | tf_op jit(solution)/shard_map/bnd,bnr->bdr/dot_general | solution.py:73
  134.9 0.0 copy-done.6
  135.0 1.5 convolution_convert_fusion.1
  136.5 0.0 copy-start.2
  136.5 2.5 %copy.44 = bf16[8,2048,64]{1,2,0:T(8,128)(2,1)} copy(bf16[8,2048,64]{1,0,2:T(8,128)(2,1)S(1)} %convolution_convert_fusion.1) | data formatting | bytes 4194304 | tf_op jit(solution)/shard_map/convert_element_type | solution.py:81
  138.9 0.0 all-to-all-done.4
  138.9 4.4 %all-to-all-start.3 = ((bf16[8,2048,64]{1,2,0:T(8,128)(2,1)}), bf16[8,2048,64]{1,2,0:T(8,128)(2,1)}, u32[]{:S(2)}, u32[]{:S(2)}) async-start(bf16[8,2048,64]{1,2,0:T(8,128)(2,1)} %copy.44), calls=%async_computation.4 | async-start | bytes 4194304 | tf_op jit(solution)/shard_map/all_to_all | solution.py:86
  143.3 0.0 copy-done.2
  143.3 0.0 copy-start.7
  143.4 4.5 %fusion.11 = f32[8,128,2048]{2,1,0:T(8,128)} fusion(bf16[8,2048,64]{1,2,0:T(8,128)(2,1)S(1)} %copy-done.2, pred[8]{0:T(512)(128)(4,1)S(1)} %get-tuple-element.22, bf16[8,128,64]{1,2,0:T(8,128)(2,1)S(1)} %get-tuple-element.21), kind=kOutput, calls=%fused_computation.25 | convolution fusion | flops 269484032 | bytes 10616840 | tf_op jit(solution)/shard_map/bnr,bdr->bnd/dot_general | solution.py:68
  147.9 0.0 copy-done.7
  147.9 0.4 convolution_multiply_fusion
  148.3 0.4 convolution_convert_fusion.3
  148.7 1.0 copy.50
  149.6 0.0 all-gather.2.cloned.1.call-done
  149.6 11.9 %fusion = bf16[1024,2048]{1,0:T(8,128)(2,1)} fusion(f32[8,128,2048]{2,1,0:T(8,128)} %fusion.11, bf16[1024,1024]{1,0:T(8,128)(2,1)} %all-gather.2.cloned.1.call-done, bf16[2048,1024]{1,0:T(8,128)(2,1)} %param.8), kind=kOutput, calls=%fused_computation.4 | convolution fusion | flops 4299161600 | bytes 18874368 | tf_op jit(solution)/shard_map/dot_general | solution.py:62
  161.5 8.4 %all-to-all-done.3 = bf16[8,2048,64]{1,2,0:T(8,128)(2,1)} async-done(((bf16[8,2048,64]{1,2,0:T(8,128)(2,1)}), bf16[8,2048,64]{1,2,0:T(8,128)(2,1)}, u32[]{:S(2)}, u32[]{:S(2)}) %all-to-all-start.3) | async-done | bytes 2097184 | tf_op jit(solution)/shard_map/all_to_all | solution.py:86
  170.0 3.3 %convolution_convert_fusion = bf16[16,2048,64]{1,0,2:T(8,128)(2,1)S(1)} fusion(bf16[8,2048,64]{1,2,0:T(8,128)(2,1)} %all-to-all-done.3, s32[8]{0:T(128)S(1)} %reduce), kind=kOutput, calls=%fused_computation.7 | convolution fusion | flops 35651712 | bytes 6291488 | tf_op jit(solution)/shard_map/sa,sdr->adr/dot_general | solution.py:89
  173.3 4.3 %copy.49 = bf16[16,2048,64]{1,2,0:T(8,128)(2,1)} copy(bf16[16,2048,64]{1,0,2:T(8,128)(2,1)S(1)} %convolution_convert_fusion) | data formatting | bytes 8388608
  177.6 0.0 reduce-scatter.2.cloned.1.call-done
  177.6 2.2 %fusion.10 = bf16[1024,256]{1,0:T(8,128)(2,1)} fusion(f32[1024,256]{1,0:T(8,128)} %reduce-scatter.2.cloned.1.call-done, f32[8,128,256]{2,1,0:T(8,128)S(1)} %convolution_multiply_fusion), kind=kLoop, calls=%fused_computation.24 | loop fusion | flops 524288 | bytes 2621440 | tf_op jit(solution)/shard_map/convert_element_type | solution.py:56
  (7 shorter events, 0.1 us)
Async XLA Ops:
  7.2 22.1 %copy-start = (bf16[16,64,256]{2,1,0:T(8,128)(2,1)S(1)}, bf16[16,64,256]{2,1,0:T(8,128)(2,1)}, u32[]{:S(2)}) copy-start(bf16[16,64,256]{2,1,0:T(8,128)(2,1)} %param.10) | copy-start | bytes 1572868
  7.2 142.5 %all-gather.2.cloned.1.call-start = ((), (), s32[]{:S(2)}) async-start(), calls=%async_computation.7 | async-start | bytes 2621440 | tf_op jit(solution)/shard_map/all_gather | solution.py:63
  7.9 169.7 %reduce-scatter.2.cloned.1.call-start = ((), (), s32[]{:S(2)}) async-start(), calls=%async_computation.6 | async-start | bytes 5242880 | tf_op jit(solution)/shard_map/reduce_scatter | solution.py:52
  17.9 0.7 copy-start.8
  17.9 0.7 copy-start.1
  30.5 12.7 %all-to-all-start.2 = ((bf16[8,64,256]{2,1,0:T(8,128)(2,1)}), bf16[8,64,256]{2,1,0:T(8,128)(2,1)S(1)}, u32[]{:S(2)}, u32[]{:S(2)}) async-start(bf16[8,64,256]{2,1,0:T(8,128)(2,1)} %copy.42), calls=%async_computation.3 | async-start | bytes 524288 | tf_op jit(solution)/shard_map/all_to_all | solution.py:44
  40.7 8.9 %copy-start.3 = (bf16[1024,256]{1,0:T(8,128)(2,1)S(1)}, bf16[1024,256]{1,0:T(8,128)(2,1)}, u32[]{:S(2)}) copy-start(bf16[1024,256]{1,0:T(8,128)(2,1)} %param.13) | copy-start | bytes 1572868
  43.2 0.7 copy-start.4
  43.9 30.8 %all-to-all-start.1 = ((bf16[8,2048,64]{1,2,0:T(8,128)(2,1)}), bf16[8,2048,64]{1,2,0:T(8,128)(2,1)S(1)}, u32[]{:S(2)}, u32[]{:S(2)}) async-start(bf16[8,2048,64]{1,2,0:T(8,128)(2,1)} %copy.40), calls=%async_computation.2 | async-start | bytes 4194304 | tf_op jit(solution)/shard_map/all_to_all | solution.py:43
  76.6 4.5 %copy-start.5 = (f32[8,128,64]{1,2,0:T(8,128)S(1)}, f32[8,128,64]{1,2,0:T(8,128)}, u32[]{:S(2)}) copy-start(f32[8,128,64]{1,2,0:T(8,128)} %fusion.9) | copy-start | bytes 786436
  127.4 7.6 %copy-start.6 = (bf16[8,128,64]{1,2,0:T(8,128)(2,1)}, bf16[8,128,64]{1,2,0:T(8,128)(2,1)S(1)}, u32[]{:S(2)}) copy-start(bf16[8,128,64]{1,2,0:T(8,128)(2,1)S(1)} %get-tuple-element.20) | copy-start | bytes 393220
  128.6 10.3 %all-to-all-start.4 = ((bf16[8,64,256]{2,1,0:T(8,128)(2,1)}), bf16[8,64,256]{2,1,0:T(8,128)(2,1)S(1)}, u32[]{:S(2)}, u32[]{:S(2)}) async-start(bf16[8,64,256]{2,1,0:T(8,128)(2,1)} %copy.47), calls=%async_computation.5 | async-start | bytes 524288 | tf_op jit(solution)/shard_map/all_to_all | solution.py:87
  136.5 6.9 %copy-start.2 = (bf16[8,2048,64]{1,2,0:T(8,128)(2,1)S(1)}, bf16[8,2048,64]{1,2,0:T(8,128)(2,1)}, u32[]{:S(2)}) copy-start(bf16[8,2048,64]{1,2,0:T(8,128)(2,1)} %gather_fusion.1) | copy-start | bytes 6291460
  138.9 31.0 %all-to-all-start.3 = ((bf16[8,2048,64]{1,2,0:T(8,128)(2,1)}), bf16[8,2048,64]{1,2,0:T(8,128)(2,1)}, u32[]{:S(2)}, u32[]{:S(2)}) async-start(bf16[8,2048,64]{1,2,0:T(8,128)(2,1)} %copy.44), calls=%async_computation.4 | async-start | bytes 4194304 | tf_op jit(solution)/shard_map/all_to_all | solution.py:86
  143.3 4.5 %copy-start.7 = (bf16[8,128,64]{1,2,0:T(8,128)(2,1)S(1)}, bf16[8,128,64]{1,2,0:T(8,128)(2,1)}, u32[]{:S(2)}) copy-start(bf16[8,128,64]{1,2,0:T(8,128)(2,1)} %copy-done.6) | copy-start | bytes 393220
Sparse Core Ops, SparseCore 0:
  9.6 48.9 all-gather.1
  60.8 91.8 reduce-scatter.1
where the time goes:
time: 187 us
  blocking collectives  55.9 us (30%)
  matrix products  48 us (26%)
  waiting for transfers between devices  33.2 us (18%)
  local copies, waits for them, and re-layouts  17.4 us (9%)
  starting transfers between devices  15.4 us (8%)
  between operations  14.2 us (8%)
  other arithmetic  2.57 us (1%)
    psum x1, blocking collectives, on_device(): low = lax.psum(low_part, 'tensor').astype(jnp.bfloat16)  46.2 us
    all_to_all x1, waiting for transfers between devices, on_device(): lax.all_to_all(reply_down, 'dp', split_axis=0, concat_axis=0, tiled=True)  24 us
    dot_general x1, matrix products, on_device(): lax.dot_general(lax.all_gather(value_gradient, 'tensor', axis=1, tiled=Tr...  11.9 us
    dot_general x1, matrix products, on_device(): jnp.dot(inputs, frozen_value_weight, preferred_element_type=jnp.float32)  9.92 us
    all_to_all x1, blocking collectives, on_device(): lax.all_to_all(wanted[:, None], 'dp', split_axis=0, concat_axis=0, tiled=...  9.62 us
    all_to_all x1, waiting for transfers between devices, on_device(): lax.all_to_all(send_down, 'dp', split_axis=0, concat_axis=0, tiled=True)  8.44 us
    dot_general x1, matrix products, on_device(): jnp.einsum('ig,gnx->inx', selected_adapter, adapter_down_weight, preferre...  6.79 us
    unnamed x20, local copies, waits for them, and re-layouts  6.64 us
  transfers between devices with their start and end apart: 6, of which 2 were waited for; matrix products, arithmetic and copies ran while one was open for 34% of the time, Pallas kernels for 0%

commit v1 on v0

v1 whole, which is shorter than its diff:
```python
import functools

import jax
import jax.numpy as jnp
from jax import lax
from jax.experimental import pallas as pl
from jax.experimental.pallas import tpu as pltpu
from jax.sharding import PartitionSpec as P

BLOCK = 128
SCALE = 0.5
BF = jnp.bfloat16
F32 = jnp.float32
VMEM_LIMIT = 48 * 1024 * 1024
ALL_VMEM = 62 * 1024 * 1024
LANES = 128

SWAP = [(0, 1), (1, 0), (2, 3), (3, 2)]
FAR_SWAP = [(0, 2), (2, 0), (1, 3), (3, 1)]


def dot(a, b, dims):
    return lax.dot_general(a, b, (dims, ((), ())), preferred_element_type=F32)


def smem():
    return pl.BlockSpec(memory_space=pltpu.SMEM)


def vmem():
    return pl.BlockSpec(memory_space=pltpu.VMEM)


def hbm():
    return pl.BlockSpec(memory_space=pltpu.HBM)


def array(shape, dtype):
    return jax.ShapeDtypeStruct(shape, dtype)


def after(x, *others):
    return lax.optimization_barrier((x,) + others)[0]


def call(kernel, name, out_shape, limit=VMEM_LIMIT, **how):
    return pl.pallas_call(
        kernel,
        out_shape=out_shape,
        compiler_params=pltpu.CompilerParams(vmem_limit_bytes=limit),
        cost_estimate=pl.CostEstimate(flops=0, bytes_accessed=0, transcendentals=0),
        name=name,
        **how,
    )


def copies():
    return pltpu.SemaphoreType.DMA


def request_kernel(nblocks, kept, count_dp, per_block_in, index_in, wanted, keeper, per_block, index, sems):
    started = (
        pltpu.make_async_copy(per_block_in, per_block, sems.at[0]),
        pltpu.make_async_copy(index_in, index, sems.at[1]),
    )
    for copy in started:
        copy.start()
    for copy in started:
        copy.wait()
    row = lax.broadcasted_iota(jnp.int32, (count_dp, 1, LANES), 0)
    value = jnp.full((count_dp, 1, LANES), -1, jnp.int32)
    for b in range(nblocks):
        spot = index[per_block[b]]
        k = lax.div(spot, kept)
        keeper[b] = k
        value = jnp.where(row == k, spot - k * kept, value)
    wanted[...] = value


def request(per_block, index, kept, count_dp):
    nblocks = per_block.shape[0]
    return call(
        functools.partial(request_kernel, nblocks, kept, count_dp),
        "request",
        (array((count_dp, 1, LANES), jnp.int32), array((nblocks,), jnp.int32)),
        in_specs=[hbm(), hbm()],
        out_specs=(vmem(), smem()),
        limit=ALL_VMEM,
        scratch_shapes=[
            pltpu.SMEM(per_block.shape, jnp.int32),
            pltpu.SMEM(index.shape, jnp.int32),
            copies()((2,)),
        ],
    )(per_block, index)


def select_kernel(count_dp, asked, source, out, held, sems):
    moves = []
    for s in range(count_dp):
        copy = pltpu.make_async_copy(
            source.at[jnp.maximum(asked[s, 0, 0], 0)], held.at[s], sems.at[0, s]
        )
        copy.start()
        moves.append((copy, pltpu.make_async_copy(held.at[s], out.at[s], sems.at[1, s])))
    for here, there in moves:
        here.wait()
        there.start()
    for here, there in moves:
        there.wait()


def select(asked, source, count_dp, name):
    shape = (count_dp,) + source.shape[1:]
    return call(
        functools.partial(select_kernel, count_dp),
        name,
        array(shape, BF),
        limit=ALL_VMEM,
        in_specs=[smem(), hbm()],
        out_specs=hbm(),
        scratch_shapes=[pltpu.VMEM(shape, BF), copies()((2, count_dp))],
    )(asked, source)


def low_gradient_kernel(nblocks, keeper, up, dy, part, sent):
    for b in range(nblocks):
        value = SCALE * dot(up[keeper[b]], dy[b * BLOCK:(b + 1) * BLOCK, :], ((1,), (1,)))
        part[b] = value
        sent[b] = value.astype(BF)


def low_gradient(keeper, up, dy):
    nblocks = keeper.shape[0]
    shape = (nblocks, up.shape[1], BLOCK)
    return call(
        functools.partial(low_gradient_kernel, nblocks),
        "low_gradient",
        (array(shape, F32), array(shape, BF)),
        in_specs=[smem(), vmem(), vmem()],
        out_specs=(vmem(), vmem()),
    )(keeper, up, dy)


def low_kernel(nblocks, keeper, down, x, part, sent, downs, xs, sems):
    started = []
    for b in range(nblocks):
        pair = (
            pltpu.make_async_copy(down.at[keeper[b]], downs.at[b], sems.at[0, b]),
            pltpu.make_async_copy(x.at[pl.ds(b * BLOCK, BLOCK)], xs.at[b], sems.at[1, b]),
        )
        for copy in pair:
            copy.start()
        started.append(pair)
    for b in range(nblocks):
        for copy in started[b]:
            copy.wait()
        value = dot(downs[b], xs[b], ((1,), (1,)))
        part[b] = value
        sent[b] = value.astype(BF)


def low_partial(keeper, down, x):
    nblocks = keeper.shape[0]
    _, rank, feat = down.shape
    shape = (nblocks, rank, BLOCK)
    return call(
        functools.partial(low_kernel, nblocks),
        "low_partial",
        (array(shape, F32), array(shape, BF)),
        in_specs=[smem(), hbm(), hbm()],
        out_specs=(vmem(), vmem()),
        scratch_shapes=[
            pltpu.VMEM((nblocks, rank, feat), BF),
            pltpu.VMEM((nblocks, BLOCK, feat), BF),
            copies()((2, nblocks)),
        ],
    )(keeper, down, x)


def total(refs, b):
    value = refs[0][b].astype(F32)
    for ref in refs[1:]:
        value = value + ref[b].astype(F32)
    return value.astype(BF)


def down_terms_kernel(nblocks, addends, keeper, *refs):
    x, terms, grad_low, xs, made, sems = refs[addends:]
    started, sent = [], []
    for b in range(nblocks):
        copy = pltpu.make_async_copy(x.at[pl.ds(b * BLOCK, BLOCK)], xs.at[b], sems.at[0, b])
        copy.start()
        started.append(copy)
    for b in range(nblocks):
        g = total(refs[:addends], b)
        grad_low[b] = g
        started[b].wait()
        made[b] = dot(g, xs[b], ((1,), (0,))).astype(BF)
        copy = pltpu.make_async_copy(made.at[b], terms.at[keeper[b]], sems.at[1, b])
        copy.start()
        sent.append(copy)
    for copy in sent:
        copy.wait()


def down_terms(keeper, grad_low, x, count_dp):
    nblocks = keeper.shape[0]
    rank = grad_low[0].shape[1]
    feat = x.shape[1]
    return call(
        functools.partial(down_terms_kernel, nblocks, len(grad_low)),
        "down_terms",
        (array((count_dp, rank, feat), BF), array((nblocks, rank, BLOCK), BF)),
        limit=ALL_VMEM,
        in_specs=[smem()] + [vmem()] * len(grad_low) + [hbm()],
        out_specs=(hbm(), vmem()),
        scratch_shapes=[
            pltpu.VMEM((nblocks, BLOCK, feat), BF),
            pltpu.VMEM((nblocks, rank, feat), BF),
            copies()((2, nblocks)),
        ],
    )(keeper, *grad_low, x)


def up_terms_kernel(nblocks, addends, keeper, *refs):
    dy, terms, low = refs[addends:]
    for b in range(nblocks):
        value = total(refs[:addends], b)
        low[b] = value
        terms[keeper[b]] = dot(
            value, dy[b * BLOCK:(b + 1) * BLOCK, :], ((1,), (0,))
        ).astype(BF)


def up_terms(keeper, low, dy, count_dp):
    nblocks = keeper.shape[0]
    rank = low[0].shape[1]
    cols = dy.shape[1]
    return call(
        functools.partial(up_terms_kernel, nblocks, len(low)),
        "up_terms",
        (array((count_dp, rank, cols), BF), array((nblocks, rank, BLOCK), BF)),
        in_specs=[smem()] + [vmem()] * (len(low) + 1),
        out_specs=(vmem(), vmem()),
    )(keeper, *low, dy)


def frozen_kernel(runs, z, x, *refs):
    ws, adds, outs = refs[:runs], refs[runs:-runs], refs[-runs:]
    for i in range(runs):
        value = dot(x[...], ws[i][...], ((1,), (0,)))
        if adds:
            value = value + adds[i][...].astype(F32)
        outs[i][...] = value.astype(outs[i].dtype)


def frozen(z, x, w, turns, width, adds, dtype, name):
    rows, feat = x.shape
    tile = 512
    runs = len(turns)
    part = pl.BlockSpec((tile, width), lambda i, z: (i, 0))
    return call(
        functools.partial(frozen_kernel, runs),
        name,
        (array((rows, width), dtype),) * runs,
        limit=ALL_VMEM,
        grid_spec=pltpu.PrefetchScalarGridSpec(
            num_scalar_prefetch=1,
            grid=(rows // tile,),
            in_specs=[pl.BlockSpec((tile, feat), lambda i, z: (i, 0))]
            + [pl.BlockSpec((feat, width), lambda i, z, t=t: (0, z[0] ^ t)) for t in turns]
            + [part] * len(adds),
            out_specs=(part,) * runs,
        ),
    )(z, x, *([w] * runs), *adds)


def values_kernel(nblocks, addends, keeper, *refs):
    low, up, out = refs[addends:]
    for b in range(nblocks):
        rows = slice(b * BLOCK, (b + 1) * BLOCK)
        value = SCALE * dot(low[b], up[keeper[b]], ((0,), (0,)))
        for ref in refs[:addends]:
            value = value + ref[rows, :].astype(F32)
        out[rows, :] = value.astype(BF)


def values_out(keeper, addends, low, up):
    return call(
        functools.partial(values_kernel, low.shape[0], len(addends)),
        "values",
        array(addends[0].shape, BF),
        in_specs=[smem()] + [vmem()] * (len(addends) + 2),
        out_specs=vmem(),
    )(keeper, *addends, low, up)


def grad_inputs_kernel(nblocks, count, z, keeper, *refs):
    pieces = refs[:count]
    w, grad_low, down, out, full = refs[count:]

    @pl.when(pl.program_id(0) == 0)
    def _():
        for turn, piece in enumerate(pieces):
            width = piece.shape[1]
            column = pl.multiple_of((z[0] ^ turn) * width, width)
            full[:, pl.ds(column, width)] = piece[...]

    base = dot(full[...], w[...], ((1,), (1,)))
    for b in range(nblocks):
        rows = slice(b * BLOCK, (b + 1) * BLOCK)
        back = dot(grad_low[b], down[keeper[b]], ((0,), (0,)))
        out[rows, :] = (base[rows, :] + back).astype(BF)


def grad_inputs_out(z, keeper, pieces, w, grad_low, down):
    nblocks, rank, _ = grad_low.shape
    count_dp = down.shape[0]
    rows = pieces[0].shape[0]
    feat, cols = w.shape
    tile = min(512, feat)
    return call(
        functools.partial(grad_inputs_kernel, nblocks, len(pieces)),
        "grad_inputs",
        array((rows, feat), BF),
        grid_spec=pltpu.PrefetchScalarGridSpec(
            num_scalar_prefetch=2,
            grid=(feat // tile,),
            in_specs=[
                pl.BlockSpec(a.shape, lambda i, s, k, n=a.ndim: (0,) * n) for a in pieces
            ]
            + [
                pl.BlockSpec((tile, cols), lambda i, s, k: (i, 0)),
                pl.BlockSpec(grad_low.shape, lambda i, s, k: (0, 0, 0)),
                pl.BlockSpec((count_dp, rank, tile), lambda i, s, k: (0, 0, i)),
            ],
            out_specs=pl.BlockSpec((rows, tile), lambda i, s, k: (0, i)),
            scratch_shapes=[pltpu.VMEM((rows, cols), BF)],
        ),
    )(z, keeper, *pieces, w, grad_low, down)


def collect_kernel(count_dp, kept, asked, terms, out, held, zeros, acc, sems, zero_sems):
    wants = [asked[s, 0, 0] for s in range(count_dp)]
    incoming = [
        pltpu.make_async_copy(terms.at[s], held.at[s], sems.at[0, s]) for s in range(count_dp)
    ]
    for copy in incoming:
        copy.start()
    zeros[...] = jnp.zeros_like(zeros)
    blank = []
    for q in range(kept):
        hits = sum((want == q).astype(jnp.int32) for want in wants)
        blank.append(hits == 0)

        @pl.when(blank[q])
        def _():
            pltpu.make_async_copy(zeros, out.at[q], zero_sems.at[q]).start()

    def send(s):
        return pltpu.make_async_copy(held.at[s], out.at[jnp.maximum(wants[s], 0)], sems.at[1, s])

    leads, shared = [], []
    for s in range(count_dp):
        earlier = jnp.int32(0)
        later = jnp.int32(0)
        for o in range(count_dp):
            same = (wants[o] == wants[s]).astype(jnp.int32)
            if o < s:
                earlier = earlier + same
            if o > s:
                later = later + same
        leads.append((wants[s] >= 0) & (earlier == 0))
        shared.append(later > 0)
        incoming[s].wait()

        @pl.when(leads[s] & ~shared[s])
        def _():
            send(s).start()

    for s in range(count_dp):
        @pl.when(leads[s] & shared[s])
        def _():
            acc[...] = held[s].astype(F32)

            @pl.loop(s + 1, count_dp)
            def _(o):
                @pl.when(asked[o, 0, 0] == wants[s])
                def _():
                    acc[...] += held[o].astype(F32)

            held[s] = acc[...].astype(BF)
            send(s).start()

    for s in range(count_dp):
        @pl.when(leads[s])
        def _():
            send(s).wait()

    for q in range(kept):
        @pl.when(blank[q])
        def _():
            pltpu.make_async_copy(zeros, out.at[q], zero_sems.at[q]).wait()


def collect(asked, terms, kept, name):
    count_dp, rank, width = terms.shape
    return call(
        functools.partial(collect_kernel, count_dp, kept),
        name,
        array((kept, rank, width), BF),
        in_specs=[smem(), hbm()],
        out_specs=hbm(),
        scratch_shapes=[
            pltpu.VMEM((count_dp, rank, width), BF),
            pltpu.VMEM((rank, width), BF),
            pltpu.VMEM((rank, width), F32),
            copies()((2, count_dp)),
            copies()((kept,)),
        ],
    )(asked, terms)


def exchange(a):
    return lax.all_to_all(a, "dp", split_axis=0, concat_axis=0, tiled=True)


def permute(a, pairs):
    return lax.ppermute(a, "tensor", pairs)


def on_line(x, w, down_kept, up_kept, per_block, index, dy):
    count_dp = lax.axis_size("dp")
    z = lax.axis_index("tensor").astype(jnp.int32)[None]
    kept = down_kept.shape[0]
    width = dy.shape[1]

    far_dy = permute(dy, FAR_SWAP)
    near_dy = permute(dy, SWAP)
    wanted, keeper = request(per_block, index, kept, count_dp)
    far_first, near_first = frozen(after(z, wanted), x, w, (3, 1), width, (), BF, "frozen_first")
    asked = exchange(wanted)
    sent_up = select(after(asked, near_first), up_kept, count_dp, "select_up")
    sent_down = select(after(asked, sent_up), down_kept, count_dp, "select_down")
    up = exchange(sent_up)
    part, sent = low_gradient(after(keeper, sent_down), up, dy)
    down = exchange(after(sent_down, part, far_dy, near_dy))

    swapped = permute(sent, SWAP)
    (own,) = frozen(after(z, part), x, w, (0,), width, (), BF, "frozen_own")
    came_far = permute(after(far_first, swapped, own), SWAP)
    part = after(part, own) + swapped
    grad_low_sum = (part, permute(part.astype(BF), FAR_SWAP))
    (far_made,) = frozen(after(z, part), x, w, (2,), width, (came_far,), BF, "frozen_far")
    sent_terms, grad_low = down_terms(after(keeper, far_made), grad_low_sum, x, count_dp)
    got_terms = exchange(sent_terms)
    near_far_dy = permute(after(far_dy, sent_terms), SWAP)

    part, sent = low_partial(after(keeper, grad_low), down, x)
    swapped = permute(sent, SWAP)
    part = part + swapped
    passed = permute(part.astype(BF), FAR_SWAP)
    far_came = permute(after(far_made, passed), FAR_SWAP)
    came_near = permute(after(near_first, passed), SWAP)
    low_sum = (part, passed)
    grad_inputs = grad_inputs_out(
        z, after(keeper, part), (dy, near_dy, far_dy, near_far_dy), w, grad_low, down
    )
    sent_up_terms, low = up_terms(after(keeper, grad_inputs), low_sum, dy, count_dp)
    got_up_terms = exchange(sent_up_terms)
    grad_down = collect(after(asked, sent_up_terms), got_terms, kept, "collect_down")
    values = values_out(after(keeper, grad_down), (own, came_near, far_came), low, up)
    grad_up = collect(after(asked, values), got_up_terms, kept, "collect_up")
    return values, grad_inputs, grad_down, grad_up


def on_ring(x, w, down_kept, up_kept, per_block, index, dy):
    count_dp = lax.axis_size("dp")
    kept = down_kept.shape[0]
    wanted, keeper = request(per_block, index, kept, count_dp)
    asked = exchange(wanted)
    up = exchange(select(asked, up_kept, count_dp, "select_up"))
    down = exchange(select(asked, down_kept, count_dp, "select_down"))
    full_dy = lax.all_gather(dy, "tensor", axis=1, tiled=True)
    none = jnp.zeros((1,), jnp.int32)
    (base,) = frozen(none, x, w, (0,), w.shape[1], (), F32, "frozen_all")
    own = lax.psum_scatter(base, "tensor", scatter_dimension=1, tiled=True)
    grad_low_sum = lax.psum(low_gradient(keeper, up, dy)[0], "tensor")
    sent_terms, grad_low = down_terms(keeper, (grad_low_sum,), x, count_dp)
    got_terms = exchange(sent_terms)
    low_sum = lax.psum(low_partial(keeper, down, x)[0], "tensor")
    sent_up_terms, low = up_terms(keeper, (low_sum,), dy, count_dp)
    got_up_terms = exchange(sent_up_terms)
    grad_inputs = grad_inputs_out(none, keeper, (full_dy,), w, grad_low, down)
    values = values_out(keeper, (own,), low, up)
    grad_down = collect(asked, got_terms, kept, "collect_down")
    grad_up = collect(asked, got_up_terms, kept, "collect_up")
    return values, grad_inputs, grad_down, grad_up


def on_device(
    inputs,
    frozen_value_weight,
    adapter_down_weight,
    adapter_up_weight,
    adapter_per_block,
    adapter_storage_index,
    value_gradient,
):
    run = on_line if lax.axis_size("tensor") == 4 else on_ring
    values, grad_inputs, grad_down, grad_up = run(
        inputs,
        frozen_value_weight,
        jnp.swapaxes(adapter_down_weight, 1, 2),
        adapter_up_weight,
        adapter_per_block,
        adapter_storage_index,
        value_gradient,
    )
    return values, grad_inputs, jnp.swapaxes(grad_down, 1, 2), grad_up


def solution(mesh):
    return jax.shard_map(
        on_device,
        mesh=mesh,
        in_specs=(
            P("dp", "tensor"),
            P("tensor", None),
            P("dp", "tensor", None),
            P("dp", None, "tensor"),
            P("dp"),
            P(),
            P("dp", "tensor"),
        ),
        out_specs=(
            P("dp", "tensor"),
            P("dp", "tensor"),
            P("dp", "tensor", None),
            P("dp", None, "tensor"),
        ),
        check_vma=False,
    )
```

time: 187 us -> 128 us (0.68)
  blocking collectives: 55.9 us -> 0 us
  Pallas kernels: 0 us -> 50.6 us
  matrix products: 48 us -> 0 us
  starting transfers between devices: 15.4 us -> 32.3 us
  local copies, waits for them, and re-layouts: 17.4 us -> 3.48 us
  between operations: 14.2 us -> 0.81 us
  waiting for transfers between devices: 33.2 us -> 37.9 us
    pallas_call x0 -> x14, Pallas kernels: none -> 50.6 us  [the longest x3 13.6 us: frozen(): call(functools.partial(frozen_kernel, runs), name, (array((rows, width),...]
    dot_general x14 -> x0, matrix products: 48 us -> none  [the longest x1 11.9 us: on_device(): lax.dot_general(lax.all_gather(value_gradient, 'tensor', axis=1, tiled=Tr...]
    psum x1 -> x0, blocking collectives: 46.2 us -> none  [on_device(): low = lax.psum(low_part, 'tensor').astype(jnp.bfloat16)]
    ppermute x0 -> x10, waiting for transfers between devices: none -> 34.6 us  [permute(): return lax.ppermute(a, 'tensor', pairs)]
    all_to_all x4 -> x5, waiting for transfers between devices: 32.5 us -> 3.26 us  [exchange(): return lax.all_to_all(a, 'dp', split_axis=0, concat_axis=0, tiled=True)]
    ppermute x0 -> x10, starting transfers between devices: none -> 12.5 us  [permute(): return lax.ppermute(a, 'tensor', pairs)]
    all_to_all x1 -> x0, blocking collectives: 9.62 us -> none  [on_device(): lax.all_to_all(wanted[:, None], 'dp', split_axis=0, concat_axis=0, tiled=...]
    convert_element_type x4 -> x0, local copies, waits for them, and re-layouts: 6.48 us -> none  [the longest x1 2.48 us: on_device(): reply_down = jnp.einsum('ig,gnx->inx', selected_adapter, adapter_down_wei...]
  transfers between devices with their start and end apart: 6 -> 15, of which waited for: 2 -> 6; matrix products, arithmetic and copies ran while one was open for 34% -> 1% of each run, Pallas kernels for 0% -> 38%
where the time goes in v1:
time: 128 us; the launch traced here: 127 us
  Pallas kernels  50.6 us (40%)
  waiting for transfers between devices  37.9 us (30%)
  starting transfers between devices  32.3 us (25%)
  local copies, waits for them, and re-layouts  3.48 us (3%)
  other arithmetic  1.83 us (1%)
    ppermute x10, waiting for transfers between devices, permute(): return lax.ppermute(a, 'tensor', pairs)  34.6 us
    all_to_all x5, starting transfers between devices, exchange(): return lax.all_to_all(a, 'dp', split_axis=0, concat_axis=0, tiled=True)  19.8 us
    pallas_call x3, Pallas kernels, frozen(): call(functools.partial(frozen_kernel, runs), name, (array((rows, width),...  13.6 us
    ppermute x10, starting transfers between devices, permute(): return lax.ppermute(a, 'tensor', pairs)  12.5 us
    pallas_call x1, Pallas kernels, grad_inputs_out(): call(functools.partial(grad_inputs_kernel, nblocks, len(pieces)), 'grad_i...  9.67 us
    pallas_call x2, Pallas kernels, select(): call(functools.partial(select_kernel, count_dp), name, array(shape, BF),...  6.08 us
    pallas_call x2, Pallas kernels, collect(): call(functools.partial(collect_kernel, count_dp, kept), name, array((kept...  5.54 us
    pallas_call x1, Pallas kernels, down_terms(): call(functools.partial(down_terms_kernel, nblocks, len(grad_low)), 'down_...  5.34 us
  transfers between devices with their start and end apart: 15, of which 6 were waited for; matrix products, arithmetic and copies ran while one was open for 1% of the time, Pallas kernels for 38%

profile of v1, /device:TPU:0, one launch (start us, length us, event | category | flops | bytes accessed | tf_op | source)
XLA Modules:
  0.0 127.0 jit_solution(8204134186746289402)
XLA Ops:
  0.6 3.1 %collective-permute-start.4 = (bf16[1024,256]{1,0:T(8,128)(2,1)}, bf16[1024,256]{1,0:T(8,128)(2,1)S(1)}, u32[]{:S(2)}, u32[]{:S(2)}) collective-permute-start(bf16[1024,256]{1,0:T(8,128)(2,1)} %refs_2_.3), channel_id=1, source_target_pairs={{0,1},{1,0},{2,3},{3,2},{4,5},{5,4},{6,7},{7,6},{8,9},{9,8},{10,11... | collective-permute-start | bytes 1572872 | tf_op jit(solution)/shard_map/ppermute | solution.py:429
  3.7 2.6 %collective-permute-start.3 = (bf16[1024,256]{1,0:T(8,128)(2,1)}, bf16[1024,256]{1,0:T(8,128)(2,1)S(1)}, u32[]{:S(2)}, u32[]{:S(2)}) collective-permute-start(bf16[1024,256]{1,0:T(8,128)(2,1)} %refs_2_.3), channel_id=1, source_target_pairs={{0,2},{2,0},{1,3},{3,1},{4,6},{6,4},{5,7},{7,5},{8,10},{10,8},{9,1... | collective-permute-start | bytes 1572872 | tf_op jit(solution)/shard_map/ppermute | solution.py:429
  6.3 1.3 %request.1 = (s32[8,1,128]{2,1,0:T(1,128)}, s32[8]{0:T(128)}) custom-call(s32[8]{0:T(128)} %per_block_in.1, s32[128]{0:T(128)} %index_in.1), custom_call_target="tpu_custom_call" | custom-call | tf_op jit(solution)/shard_map/request/pallas_call | solution.py:82
  7.6 3.7 %all-to-all-start = ((s32[8,1,128]{2,1,0:T(1,128)}), s32[8,1,128]{2,1,0:T(1,128)S(1)}, u32[]{:S(2)}, u32[]{:S(2)}) async-start(s32[8,1,128]{2,1,0:T(1,128)} %get-tuple-element.36), calls=%async_computation | async-start | bytes 8192 | tf_op jit(solution)/shard_map/all_to_all | solution.py:425
  11.4 5.5 %frozen_first.1 = (bf16[1024,256]{1,0:T(8,128)(2,1)}, bf16[1024,256]{1,0:T(8,128)(2,1)}) custom-call(s32[1]{0:T(128)} %bitcast.z, bf16[1024,2048]{1,0:T(8,128)(2,1)} %x.7, bf16[2048,1024]{1,0:T(8,128)(2,1)} %refs_4_.1, bf16[2048,1024]{1,0:T(8,128)(2,1)} %refs_4_.1), custom_call_target="tpu_custom_call" | custom-call | tf_op jit(solution)/shard_map/frozen_first/pallas_call | solution.py:262
  16.9 0.0 copy-start
  16.9 0.0 copy-start.9
  16.9 0.0 all-to-all-done.asked
  16.9 0.0 copy-start.7
  16.9 0.6 copy-done.7
  17.5 2.4 %select_up.1 = bf16[8,64,256]{2,1,0:T(8,128)(2,1)} custom-call(s32[8,1,128]{2,1,0:T(1,128)} %copy-done.7, bf16[16,64,256]{2,1,0:T(8,128)(2,1)} %source.1), custom_call_target="tpu_custom_call" | custom-call | tf_op jit(solution)/shard_map/select_up/pallas_call | solution.py:114
  19.9 4.2 %all-to-all-start.1 = ((bf16[8,64,256]{2,1,0:T(8,128)(2,1)}), bf16[8,64,256]{2,1,0:T(8,128)(2,1)S(1)}, u32[]{:S(2)}, u32[]{:S(2)}) async-start(bf16[8,64,256]{2,1,0:T(8,128)(2,1)} %select_up.1), calls=%async_computation.1 | async-start | bytes 524288 | tf_op jit(solution)/shard_map/all_to_all | solution.py:425
  24.1 3.7 %select_down.1 = bf16[8,64,2048]{2,1,0:T(8,128)(2,1)} custom-call(s32[8,1,128]{2,1,0:T(1,128)} %copy-done.7, bf16[16,64,2048]{2,1,0:T(8,128)(2,1)} %bitcast.3), custom_call_target="tpu_custom_call" | custom-call | tf_op jit(solution)/shard_map/select_down/pallas_call | solution.py:114
  27.8 3.2 %all-to-all-done.1.up.refs_4_ = bf16[8,64,256]{2,1,0:T(8,128)(2,1)S(1)} async-done(((bf16[8,64,256]{2,1,0:T(8,128)(2,1)}), bf16[8,64,256]{2,1,0:T(8,128)(2,1)S(1)}, u32[]{:S(2)}, u32[]{:S(2)}) %all-to-all-start.1) | async-done | bytes 262176 | tf_op jit(solution)/shard_map/all_to_all | solution.py:425
  31.0 0.0 copy-done
  31.0 0.0 copy-done.9
  31.0 0.8 low_gradient.1
  31.9 0.7 copy-done.4
  32.6 0.0 collective-permute-done.4.refs_1_
  32.6 0.0 collective-permute-done.3.refs_2_
  32.6 4.4 %all-to-all-start.2 = ((bf16[8,64,2048]{2,1,0:T(8,128)(2,1)}), bf16[8,64,2048]{2,1,0:T(8,128)(2,1)}, u32[]{:S(2)}, u32[]{:S(2)}) async-start(bf16[8,64,2048]{2,1,0:T(8,128)(2,1)} %select_down.1), calls=%async_computation.2 | async-start | bytes 4194304 | tf_op jit(solution)/shard_map/all_to_all | solution.py:425
  37.0 0.5 collective-permute-start
  37.5 4.0 %frozen_own.1.refs_0_ = bf16[1024,256]{1,0:T(8,128)(2,1)} custom-call(s32[1]{0:T(128)} %bitcast.z, bf16[1024,2048]{1,0:T(8,128)(2,1)} %x.7, bf16[2048,1024]{1,0:T(8,128)(2,1)} %refs_4_.1), custom_call_target="tpu_custom_call" | custom-call | tf_op jit(solution)/shard_map/frozen_own/pallas_call | solution.py:262
  41.5 0.0 copy-done.2
  41.5 1.4 %collective-permute-done = bf16[8,64,128]{2,1,0:T(8,128)(2,1)} collective-permute-done((bf16[8,64,128]{2,1,0:T(8,128)(2,1)S(1)}, bf16[8,64,128]{2,1,0:T(8,128)(2,1)}, u32[]{:S(2)}, u32[]{:S(2)}) %collective-permute-start) | collective-permute-done | bytes 131104 | tf_op jit(solution)/shard_map/ppermute | solution.py:429
  42.9 0.5 collective-permute-start.1
  43.3 1.8 %fusion.1 = (bf16[8,64,128]{2,1,0:T(8,128)(2,1)}, f32[8,64,128]{2,1,0:T(8,128)}) fusion(f32[8,64,128]{2,1,0:T(8,128)} %copy-done.4, bf16[8,64,128]{2,1,0:T(8,128)(2,1)} %collective-permute-done), kind=kLoop, calls=%fused_computation.3 | loop fusion | flops 196608 | bytes 786432 | tf_op jit(solution)/shard_map/convert_element_type | solution.py:453
  45.1 0.3 collective-permute-start.2
  45.5 13.8 %collective-permute-done.1.refs_1_ = bf16[1024,256]{1,0:T(8,128)(2,1)S(1)} collective-permute-done((bf16[1024,256]{1,0:T(8,128)(2,1)}, bf16[1024,256]{1,0:T(8,128)(2,1)S(1)}, u32[]{:S(2)}, u32[]{:S(2)}) %collective-permute-start.1) | collective-permute-done | bytes 524320 | tf_op jit(solution)/shard_map/ppermute | solution.py:429
  59.2 0.8 copy-done.11
  60.0 4.1 %frozen_far.1 = bf16[1024,256]{1,0:T(8,128)(2,1)} custom-call(s32[1]{0:T(128)} %bitcast.z, bf16[1024,2048]{1,0:T(8,128)(2,1)} %x.7, bf16[2048,1024]{1,0:T(8,128)(2,1)} %refs_4_.1, bf16[1024,256]{1,0:T(8,128)(2,1)} %copy-done.11), custom_call_target="tpu_custom_call" | custom-call | tf_op jit(solution)/shard_map/frozen_far/pallas_call | solution.py:262
  64.1 0.0 collective-permute-done.2.refs_1_
  64.1 0.0 copy-start.12
  64.2 0.6 copy-done.12
  64.8 5.3 %down_terms.1 = (bf16[8,64,2048]{2,1,0:T(8,128)(2,1)}, bf16[8,64,128]{2,1,0:T(8,128)(2,1)}) custom-call(s32[8]{0:T(128)} %get-tuple-element.61.keeper, f32[8,64,128]{2,1,0:T(8,128)} %get-tuple-element.69.refs_0_, bf16[8,64,128]{2,1,0:T(8,128)(2,1)} %copy-done.12, bf16[1024,2048]{1,0:T(8,128)(2,1)} %x.7), custom_call_target="tpu_custom_call" | custom-call | tf_op jit(solution)/shard_map/down_terms/pallas_call | solution.py:210
  70.2 0.0 all-to-all-done.2.down.refs_6_
  70.2 3.7 %all-to-all-start.3 = ((bf16[8,64,2048]{2,1,0:T(8,128)(2,1)}), bf16[8,64,2048]{2,1,0:T(8,128)(2,1)S(1)}, u32[]{:S(2)}, u32[]{:S(2)}) async-start(bf16[8,64,2048]{2,1,0:T(8,128)(2,1)} %get-tuple-element.56), calls=%async_computation.3 | async-start | bytes 4194304 | tf_op jit(solution)/shard_map/all_to_all | solution.py:425
  73.9 0.0 copy-start.6
  73.9 0.0 copy-done.10
  73.9 5.0 %low_partial.1 = (f32[8,64,128]{2,1,0:T(8,128)S(1)}, bf16[8,64,128]{2,1,0:T(8,128)(2,1)S(1)}) custom-call(s32[8]{0:T(128)S(1)} %copy-done.10, bf16[8,64,2048]{2,1,0:T(8,128)(2,1)} %all-to-all-done.2.down.refs_6_, bf16[1024,2048]{1,0:T(8,128)(2,1)} %x.7), custom_call_target="tpu_custom_call" | custom-call | tf_op jit(solution)/shard_map/low_partial/pallas_call | solution.py:166
  78.9 0.1 collective-permute-start.5
  79.0 0.0 copy-done.3
  79.0 2.0 %collective-permute-start.6 = (bf16[1024,256]{1,0:T(8,128)(2,1)S(1)}, bf16[1024,256]{1,0:T(8,128)(2,1)S(1)}, u32[]{:S(2)}, u32[]{:S(2)}) collective-permute-start(bf16[1024,256]{1,0:T(8,128)(2,1)S(1)} %copy-done.3), channel_id=1, source_target_pairs={{0,1},{1,0},{2,3},{3,2},{4,5},{5,4},{6,7},{7,6},{8,9},{9,8},{10,11... | collective-permute-start | bytes 1572872 | tf_op jit(solution)/shard_map/ppermute | solution.py:429
  81.0 4.3 %collective-permute-done.5 = bf16[8,64,128]{2,1,0:T(8,128)(2,1)S(1)} collective-permute-done((bf16[8,64,128]{2,1,0:T(8,128)(2,1)S(1)}, bf16[8,64,128]{2,1,0:T(8,128)(2,1)S(1)}, u32[]{:S(2)}, u32[]{:S(2)}) %collective-permute-start.5) | collective-permute-done | bytes 131104 | tf_op jit(solution)/shard_map/ppermute | solution.py:429
  85.3 0.1 collective-permute-start.7
  85.4 11.3 %collective-permute-done.7.refs_1_ = bf16[8,64,128]{2,1,0:T(8,128)(2,1)S(1)} collective-permute-done((bf16[8,64,128]{2,1,0:T(8,128)(2,1)S(1)}, bf16[8,64,128]{2,1,0:T(8,128)(2,1)S(1)}, u32[]{:S(2)}, u32[]{:S(2)}) %collective-permute-start.7) | collective-permute-done | bytes 131104 | tf_op jit(solution)/shard_map/ppermute | solution.py:429
  96.7 1.8 %collective-permute-start.8 = (bf16[1024,256]{1,0:T(8,128)(2,1)}, bf16[1024,256]{1,0:T(8,128)(2,1)}, u32[]{:S(2)}, u32[]{:S(2)}) collective-permute-start(bf16[1024,256]{1,0:T(8,128)(2,1)} %get-tuple-element.62), channel_id=1, source_target_pairs={{0,1},{1,0},{2,3},{3,2},{4,5},{5,4},{6,7},{7,6},{8,9},{9,8},{10,11... | collective-permute-start | bytes 1572872 | tf_op jit(solution)/shard_map/ppermute | solution.py:429
  98.5 1.6 %collective-permute-start.9 = (bf16[1024,256]{1,0:T(8,128)(2,1)}, bf16[1024,256]{1,0:T(8,128)(2,1)}, u32[]{:S(2)}, u32[]{:S(2)}) collective-permute-start(bf16[1024,256]{1,0:T(8,128)(2,1)} %frozen_far.1), channel_id=1, source_target_pairs={{0,2},{2,0},{1,3},{3,1},{4,6},{6,4},{5,7},{7,5},{8,10},{10,8},{9,1... | collective-permute-start | bytes 1572872 | tf_op jit(solution)/shard_map/ppermute | solution.py:429
  100.1 0.0 collective-permute-done.6.refs_3_
  100.1 0.0 copy-done.6
  100.1 9.7 %grad_inputs.1 = bf16[1024,2048]{1,0:T(8,128)(2,1)} custom-call(s32[1]{0:T(128)} %bitcast.z, s32[8]{0:T(128)S(1)} %copy-done.10, bf16[1024,256]{1,0:T(8,128)(2,1)S(1)} %copy-done, bf16[1024,256]{1,0:T(8,128)(2,1)S(1)} %collective-permute-done.4.refs_1_, bf16[1024,256]{1,0:T(8,128)(2,1)S(1)} %copy-done.3, ...), custom_call_target="tpu_custom_call" | custom-call | tf_op jit(solution)/shard_map/grad_inputs/pallas_call | solution.py:322
  109.8 0.8 up_terms.1
  110.6 0.0 copy-start.5
  110.6 0.7 copy-done.5
  111.3 0.0 all-to-all-done.3.terms
  111.3 3.8 %all-to-all-start.4 = ((bf16[8,64,256]{2,1,0:T(8,128)(2,1)}), bf16[8,64,256]{2,1,0:T(8,128)(2,1)S(1)}, u32[]{:S(2)}, u32[]{:S(2)}) async-start(bf16[8,64,256]{2,1,0:T(8,128)(2,1)} %copy-done.5), calls=%async_computation.4 | async-start | bytes 524288 | tf_op jit(solution)/shard_map/all_to_all | solution.py:425
  115.1 0.0 copy-done.8
  115.1 3.1 %collect_down.1 = bf16[16,64,2048]{2,1,0:T(8,128)(2,1)} custom-call(s32[8,1,128]{2,1,0:T(1,128)S(1)} %copy-done.8, bf16[8,64,2048]{2,1,0:T(8,128)(2,1)S(1)} %all-to-all-done.3.terms), custom_call_target="tpu_custom_call" | custom-call | tf_op jit(solution)/shard_map/collect_down/pallas_call | solution.py:408
  118.2 3.9 %collective-permute-done.8.refs_1_ = bf16[1024,256]{1,0:T(8,128)(2,1)} collective-permute-done((bf16[1024,256]{1,0:T(8,128)(2,1)}, bf16[1024,256]{1,0:T(8,128)(2,1)}, u32[]{:S(2)}, u32[]{:S(2)}) %collective-permute-start.8) | collective-permute-done | bytes 524320 | tf_op jit(solution)/shard_map/ppermute | solution.py:429
  122.1 0.0 collective-permute-done.9.refs_2_
  122.1 0.0 copy-done.1
  122.1 2.5 %values.1 = bf16[1024,256]{1,0:T(8,128)(2,1)} custom-call(s32[8]{0:T(128)S(1)} %copy-done.10, bf16[1024,256]{1,0:T(8,128)(2,1)S(1)} %copy-done.1, bf16[1024,256]{1,0:T(8,128)(2,1)} %collective-permute-done.8.refs_1_, bf16[1024,256]{1,0:T(8,128)(2,1)} %collective-permute-done.9.refs_2_, bf16[8,64,128]{2,1,0:T(8,128)(2,1)S(1)} %get-tuple-element.64.refs_3_, ...), custom_call_target="tpu_custom_call" | custom-call | tf_op jit(solution)/shard_map/values/pallas_call | solution.py:289
  124.5 0.0 all-to-all-done.4.terms
  124.5 2.4 %collect_up.1 = bf16[16,64,256]{2,1,0:T(8,128)(2,1)} custom-call(s32[8,1,128]{2,1,0:T(1,128)S(1)} %copy-done.8, bf16[8,64,256]{2,1,0:T(8,128)(2,1)S(1)} %all-to-all-done.4.terms), custom_call_target="tpu_custom_call" | custom-call | tf_op jit(solution)/shard_map/collect_up/pallas_call | solution.py:408
  (8 shorter events, 0.0 us)
Async XLA Ops:
  0.6 32.0 %collective-permute-start.4 = (bf16[1024,256]{1,0:T(8,128)(2,1)}, bf16[1024,256]{1,0:T(8,128)(2,1)S(1)}, u32[]{:S(2)}, u32[]{:S(2)}) collective-permute-start(bf16[1024,256]{1,0:T(8,128)(2,1)} %refs_2_.3), channel_id=1, source_target_pairs={{0,1},{1,0},{2,3},{3,2},{4,5},{5,4},{6,7},{7,6},{8,9},{9,8},{10,11... | collective-permute-start | bytes 1572872 | tf_op jit(solution)/shard_map/ppermute | solution.py:429
  3.7 28.9 %collective-permute-start.3 = (bf16[1024,256]{1,0:T(8,128)(2,1)}, bf16[1024,256]{1,0:T(8,128)(2,1)S(1)}, u32[]{:S(2)}, u32[]{:S(2)}) collective-permute-start(bf16[1024,256]{1,0:T(8,128)(2,1)} %refs_2_.3), channel_id=1, source_target_pairs={{0,2},{2,0},{1,3},{3,1},{4,6},{6,4},{5,7},{7,5},{8,10},{10,8},{9,1... | collective-permute-start | bytes 1572872 | tf_op jit(solution)/shard_map/ppermute | solution.py:429
  7.6 9.3 %all-to-all-start = ((s32[8,1,128]{2,1,0:T(1,128)}), s32[8,1,128]{2,1,0:T(1,128)S(1)}, u32[]{:S(2)}, u32[]{:S(2)}) async-start(s32[8,1,128]{2,1,0:T(1,128)} %get-tuple-element.36), calls=%async_computation | async-start | bytes 8192 | tf_op jit(solution)/shard_map/all_to_all | solution.py:425
  16.9 14.2 %copy-start = (bf16[1024,256]{1,0:T(8,128)(2,1)S(1)}, bf16[1024,256]{1,0:T(8,128)(2,1)}, u32[]{:S(2)}) copy-start(bf16[1024,256]{1,0:T(8,128)(2,1)} %refs_2_.3) | copy-start | bytes 1572868
  16.9 14.2 %copy-start.9 = (s32[8]{0:T(128)S(1)}, s32[8]{0:T(128)}, u32[]{:S(2)}) copy-start(s32[8]{0:T(128)} %get-tuple-element.61.keeper) | copy-start | bytes 100
  16.9 0.6 copy-start.7
  19.9 11.1 %all-to-all-start.1 = ((bf16[8,64,256]{2,1,0:T(8,128)(2,1)}), bf16[8,64,256]{2,1,0:T(8,128)(2,1)S(1)}, u32[]{:S(2)}, u32[]{:S(2)}) async-start(bf16[8,64,256]{2,1,0:T(8,128)(2,1)} %select_up.1), calls=%async_computation.1 | async-start | bytes 524288 | tf_op jit(solution)/shard_map/all_to_all | solution.py:425
  31.9 0.7 copy-start.4
  32.6 8.9 %copy-start.2 = (bf16[1024,256]{1,0:T(8,128)(2,1)}, bf16[1024,256]{1,0:T(8,128)(2,1)S(1)}, u32[]{:S(2)}) copy-start(bf16[1024,256]{1,0:T(8,128)(2,1)S(1)} %collective-permute-done.3.refs_2_) | copy-start | bytes 1572868
  32.6 37.5 %all-to-all-start.2 = ((bf16[8,64,2048]{2,1,0:T(8,128)(2,1)}), bf16[8,64,2048]{2,1,0:T(8,128)(2,1)}, u32[]{:S(2)}, u32[]{:S(2)}) async-start(bf16[8,64,2048]{2,1,0:T(8,128)(2,1)} %select_down.1), calls=%async_computation.2 | async-start | bytes 4194304 | tf_op jit(solution)/shard_map/all_to_all | solution.py:425
  37.0 5.9 %collective-permute-start = (bf16[8,64,128]{2,1,0:T(8,128)(2,1)S(1)}, bf16[8,64,128]{2,1,0:T(8,128)(2,1)}, u32[]{:S(2)}, u32[]{:S(2)}) collective-permute-start(bf16[8,64,128]{2,1,0:T(8,128)(2,1)S(1)} %get-tuple-element.45), channel_id=1, source_target_pairs={{0,1},{1,0},{2,3},{3,2},{4,5},{5,4},{6,7},{7,6},{8,9},{9,8},{10,11... | collective-permute-start | bytes 393224 | tf_op jit(solution)/shard_map/ppermute | solution.py:429
  42.9 16.3 %collective-permute-start.1 = (bf16[1024,256]{1,0:T(8,128)(2,1)}, bf16[1024,256]{1,0:T(8,128)(2,1)S(1)}, u32[]{:S(2)}, u32[]{:S(2)}) collective-permute-start(bf16[1024,256]{1,0:T(8,128)(2,1)} %get-tuple-element.48), channel_id=1, source_target_pairs={{0,1},{1,0},{2,3},{3,2},{4,5},{5,4},{6,7},{7,6},{8,9},{9,8},{10,11... | collective-permute-start | bytes 1572872 | tf_op jit(solution)/shard_map/ppermute | solution.py:429
  45.1 19.0 %collective-permute-start.2 = (bf16[8,64,128]{2,1,0:T(8,128)(2,1)}, bf16[8,64,128]{2,1,0:T(8,128)(2,1)S(1)}, u32[]{:S(2)}, u32[]{:S(2)}) collective-permute-start(bf16[8,64,128]{2,1,0:T(8,128)(2,1)} %get-tuple-element.68), channel_id=1, source_target_pairs={{0,2},{2,0},{1,3},{3,1},{4,6},{6,4},{5,7},{7,5},{8,10},{10,8},{9,1... | collective-permute-start | bytes 393224 | tf_op jit(solution)/shard_map/ppermute | solution.py:429
  59.2 0.8 copy-start.11
  64.1 9.7 %copy-start.10 = (s32[8]{0:T(128)S(1)}, s32[8]{0:T(128)}, u32[]{:S(2)}) copy-start(s32[8]{0:T(128)} %get-tuple-element.61.keeper) | copy-start | bytes 100
  64.1 0.7 copy-start.12
  70.2 41.1 %all-to-all-start.3 = ((bf16[8,64,2048]{2,1,0:T(8,128)(2,1)}), bf16[8,64,2048]{2,1,0:T(8,128)(2,1)S(1)}, u32[]{:S(2)}, u32[]{:S(2)}) async-start(bf16[8,64,2048]{2,1,0:T(8,128)(2,1)} %get-tuple-element.56), calls=%async_computation.3 | async-start | bytes 4194304 | tf_op jit(solution)/shard_map/all_to_all | solution.py:425
  73.9 5.2 %copy-start.3 = (bf16[1024,256]{1,0:T(8,128)(2,1)S(1)}, bf16[1024,256]{1,0:T(8,128)(2,1)}, u32[]{:S(2)}) copy-start(bf16[1024,256]{1,0:T(8,128)(2,1)} %copy-done.2) | copy-start | bytes 1572868
  73.9 26.3 %copy-start.6 = (bf16[8,64,128]{2,1,0:T(8,128)(2,1)S(1)}, bf16[8,64,128]{2,1,0:T(8,128)(2,1)}, u32[]{:S(2)}) copy-start(bf16[8,64,128]{2,1,0:T(8,128)(2,1)} %get-tuple-element.50.refs_5_) | copy-start | bytes 393220
  78.9 6.4 %collective-permute-start.5 = (bf16[8,64,128]{2,1,0:T(8,128)(2,1)S(1)}, bf16[8,64,128]{2,1,0:T(8,128)(2,1)S(1)}, u32[]{:S(2)}, u32[]{:S(2)}) collective-permute-start(bf16[8,64,128]{2,1,0:T(8,128)(2,1)S(1)} %get-tuple-element.54), channel_id=1, source_target_pairs={{0,1},{1,0},{2,3},{3,2},{4,5},{5,4},{6,7},{7,6},{8,9},{9,8},{10,11... | collective-permute-start | bytes 393224 | tf_op jit(solution)/shard_map/ppermute | solution.py:429
  79.0 21.1 %collective-permute-start.6 = (bf16[1024,256]{1,0:T(8,128)(2,1)S(1)}, bf16[1024,256]{1,0:T(8,128)(2,1)S(1)}, u32[]{:S(2)}, u32[]{:S(2)}) collective-permute-start(bf16[1024,256]{1,0:T(8,128)(2,1)S(1)} %copy-done.3), channel_id=1, source_target_pairs={{0,1},{1,0},{2,3},{3,2},{4,5},{5,4},{6,7},{7,6},{8,9},{9,8},{10,11... | collective-permute-start | bytes 1572872 | tf_op jit(solution)/shard_map/ppermute | solution.py:429
  85.3 11.4 %collective-permute-start.7 = (bf16[8,64,128]{2,1,0:T(8,128)(2,1)S(1)}, bf16[8,64,128]{2,1,0:T(8,128)(2,1)S(1)}, u32[]{:S(2)}, u32[]{:S(2)}) collective-permute-start(bf16[8,64,128]{2,1,0:T(8,128)(2,1)S(1)} %get-tuple-element.66), channel_id=1, source_target_pairs={{0,2},{2,0},{1,3},{3,1},{4,6},{6,4},{5,7},{7,5},{8,10},{10,8},{9,1... | collective-permute-start | bytes 393224 | tf_op jit(solution)/shard_map/ppermute | solution.py:429
  96.7 25.3 %collective-permute-start.8 = (bf16[1024,256]{1,0:T(8,128)(2,1)}, bf16[1024,256]{1,0:T(8,128)(2,1)}, u32[]{:S(2)}, u32[]{:S(2)}) collective-permute-start(bf16[1024,256]{1,0:T(8,128)(2,1)} %get-tuple-element.62), channel_id=1, source_target_pairs={{0,1},{1,0},{2,3},{3,2},{4,5},{5,4},{6,7},{7,6},{8,9},{9,8},{10,11... | collective-permute-start | bytes 1572872 | tf_op jit(solution)/shard_map/ppermute | solution.py:429
  98.5 23.6 %collective-permute-start.9 = (bf16[1024,256]{1,0:T(8,128)(2,1)}, bf16[1024,256]{1,0:T(8,128)(2,1)}, u32[]{:S(2)}, u32[]{:S(2)}) collective-permute-start(bf16[1024,256]{1,0:T(8,128)(2,1)} %frozen_far.1), channel_id=1, source_target_pairs={{0,2},{2,0},{1,3},{3,1},{4,6},{6,4},{5,7},{7,5},{8,10},{10,8},{9,1... | collective-permute-start | bytes 1572872 | tf_op jit(solution)/shard_map/ppermute | solution.py:429
  100.1 15.0 %copy-start.8 = (s32[8,1,128]{2,1,0:T(1,128)S(1)}, s32[8,1,128]{2,1,0:T(1,128)}, u32[]{:S(2)}) copy-start(s32[8,1,128]{2,1,0:T(1,128)} %copy-done.7) | copy-start | bytes 12292
  109.8 12.3 %copy-start.1 = (bf16[1024,256]{1,0:T(8,128)(2,1)S(1)}, bf16[1024,256]{1,0:T(8,128)(2,1)}, u32[]{:S(2)}) copy-start(bf16[1024,256]{1,0:T(8,128)(2,1)} %frozen_own.1.refs_0_) | copy-start | bytes 1572868
  110.6 0.7 copy-start.5
  111.3 13.3 %all-to-all-start.4 = ((bf16[8,64,256]{2,1,0:T(8,128)(2,1)}), bf16[8,64,256]{2,1,0:T(8,128)(2,1)S(1)}, u32[]{:S(2)}, u32[]{:S(2)}) async-start(bf16[8,64,256]{2,1,0:T(8,128)(2,1)} %copy-done.5), calls=%async_computation.4 | async-start | bytes 524288 | tf_op jit(solution)/shard_map/all_to_all | solution.py:425

commit v2 on v1

--- a/solution.py
+++ b/solution.py
@@ -12,7 +12,7 @@
 BF = jnp.bfloat16
 F32 = jnp.float32
 VMEM_LIMIT = 48 * 1024 * 1024
-ALL_VMEM = 62 * 1024 * 1024
+ALL_VMEM = 57 * 1024 * 1024
 LANES = 128
 
 SWAP = [(0, 1), (1, 0), (2, 3), (3, 2)]
@@ -273,26 +273,6 @@
             out_specs=(part,) * runs,
         ),
     )(z, x, *([w] * runs), *adds)
-
-
-def values_kernel(nblocks, addends, keeper, *refs):
-    low, up, out = refs[addends:]
-    for b in range(nblocks):
-        rows = slice(b * BLOCK, (b + 1) * BLOCK)
-        value = SCALE * dot(low[b], up[keeper[b]], ((0,), (0,)))
-        for ref in refs[:addends]:
-            value = value + ref[rows, :].astype(F32)
-        out[rows, :] = value.astype(BF)
-
-
-def values_out(keeper, addends, low, up):
-    return call(
-        functools.partial(values_kernel, low.shape[0], len(addends)),
-        "values",
-        array(addends[0].shape, BF),
-        in_specs=[smem()] + [vmem()] * (len(addends) + 2),
-        out_specs=vmem(),
-    )(keeper, *addends, low, up)
 
 
 def grad_inputs_kernel(nblocks, count, z, keeper, *refs):
@@ -340,7 +320,7 @@
     )(z, keeper, *pieces, w, grad_low, down)
 
 
-def collect_kernel(count_dp, kept, asked, terms, out, held, zeros, acc, sems, zero_sems):
+def collect_body(count_dp, kept, asked, terms, out, held, zeros, acc, sems, zero_sems, beside):
     wants = [asked[s, 0, 0] for s in range(count_dp)]
     incoming = [
         pltpu.make_async_copy(terms.at[s], held.at[s], sems.at[0, s]) for s in range(count_dp)
@@ -356,6 +336,8 @@
         @pl.when(blank[q])
         def _():
             pltpu.make_async_copy(zeros, out.at[q], zero_sems.at[q]).start()
+
+    beside()
 
     def send(s):
         return pltpu.make_async_copy(held.at[s], out.at[jnp.maximum(wants[s], 0)], sems.at[1, s])
@@ -403,6 +385,21 @@
             pltpu.make_async_copy(zeros, out.at[q], zero_sems.at[q]).wait()
 
 
+def collect_kernel(count_dp, kept, asked, terms, out, *scratch):
+    collect_body(count_dp, kept, asked, terms, out, *scratch, beside=lambda: None)
+
+
+def collect_scratch(terms, kept):
+    count_dp, rank, width = terms.shape
+    return [
+        pltpu.VMEM((count_dp, rank, width), BF),
+        pltpu.VMEM((rank, width), BF),
+        pltpu.VMEM((rank, width), F32),
+        copies()((2, count_dp)),
+        copies()((kept,)),
+    ]
+
+
 def collect(asked, terms, kept, name):
     count_dp, rank, width = terms.shape
     return call(
@@ -411,14 +408,34 @@
         array((kept, rank, width), BF),
         in_specs=[smem(), hbm()],
         out_specs=hbm(),
-        scratch_shapes=[
-            pltpu.VMEM((count_dp, rank, width), BF),
-            pltpu.VMEM((rank, width), BF),
-            pltpu.VMEM((rank, width), F32),
-            copies()((2, count_dp)),
-            copies()((kept,)),
-        ],
+        scratch_shapes=collect_scratch(terms, kept),
     )(asked, terms)
+
+
+def values_kernel(nblocks, addends, count_dp, kept, asked, keeper, terms, *refs):
+    low, up, out, sums = refs[addends:addends + 4]
+
+    def values():
+        for b in range(nblocks):
+            rows = slice(b * BLOCK, (b + 1) * BLOCK)
+            value = SCALE * dot(low[b], up[keeper[b]], ((0,), (0,)))
+            for ref in refs[:addends]:
+                value = value + ref[rows, :].astype(F32)
+            out[rows, :] = value.astype(BF)
+
+    collect_body(count_dp, kept, asked, terms, sums, *refs[addends + 4:], beside=values)
+
+
+def values_out(asked, keeper, terms, kept, addends, low, up):
+    count_dp, rank, width = terms.shape
+    return call(
+        functools.partial(values_kernel, low.shape[0], len(addends), count_dp, kept),
+        "values",
+        (array(addends[0].shape, BF), array((kept, rank, width), BF)),
+        in_specs=[smem(), smem(), hbm()] + [vmem()] * (len(addends) + 2),
+        out_specs=(vmem(), hbm()),
+        scratch_shapes=collect_scratch(terms, kept),
+    )(asked, keeper, terms, *addends, low, up)
 
 
 def exchange(a):
@@ -438,9 +455,8 @@
     far_dy = permute(dy, FAR_SWAP)
     near_dy = permute(dy, SWAP)
     wanted, keeper = request(per_block, index, kept, count_dp)
-    far_first, near_first = frozen(after(z, wanted), x, w, (3, 1), width, (), BF, "frozen_first")
     asked = exchange(wanted)
-    sent_up = select(after(asked, near_first), up_kept, count_dp, "select_up")
+    sent_up = select(asked, up_kept, count_dp, "select_up")
     sent_down = select(after(asked, sent_up), down_kept, count_dp, "select_down")
     up = exchange(sent_up)
     part, sent = low_gradient(after(keeper, sent_down), up, dy)
@@ -448,29 +464,32 @@
 
     swapped = permute(sent, SWAP)
     (own,) = frozen(after(z, part), x, w, (0,), width, (), BF, "frozen_own")
-    came_far = permute(after(far_first, swapped, own), SWAP)
     part = after(part, own) + swapped
-    grad_low_sum = (part, permute(part.astype(BF), FAR_SWAP))
-    (far_made,) = frozen(after(z, part), x, w, (2,), width, (came_far,), BF, "frozen_far")
-    sent_terms, grad_low = down_terms(after(keeper, far_made), grad_low_sum, x, count_dp)
-    got_terms = exchange(sent_terms)
-    near_far_dy = permute(after(far_dy, sent_terms), SWAP)
+    passed = permute(part.astype(BF), FAR_SWAP)
+    grad_low_sum = (part, passed)
+    far_first, near_first = frozen(after(z, part), x, w, (3, 1), width, (), BF, "frozen_first")
+    came_far = permute(after(far_first, passed), SWAP)
+    sent_terms, grad_low = down_terms(after(keeper, near_first), grad_low_sum, x, count_dp)
 
     part, sent = low_partial(after(keeper, grad_low), down, x)
     swapped = permute(sent, SWAP)
+    got_terms = exchange(after(sent_terms, part, came_far))
+    near_far_dy = permute(after(far_dy, part), SWAP)
     part = part + swapped
     passed = permute(part.astype(BF), FAR_SWAP)
-    far_came = permute(after(far_made, passed), FAR_SWAP)
+    (far_made,) = frozen(after(z, part), x, w, (2,), width, (came_far,), BF, "frozen_far")
+    far_came = permute(far_made, FAR_SWAP)
     came_near = permute(after(near_first, passed), SWAP)
     low_sum = (part, passed)
     grad_inputs = grad_inputs_out(
-        z, after(keeper, part), (dy, near_dy, far_dy, near_far_dy), w, grad_low, down
+        z, after(keeper, far_made), (dy, near_dy, far_dy, near_far_dy), w, grad_low, down
     )
     sent_up_terms, low = up_terms(after(keeper, grad_inputs), low_sum, dy, count_dp)
     got_up_terms = exchange(sent_up_terms)
     grad_down = collect(after(asked, sent_up_terms), got_terms, kept, "collect_down")
-    values = values_out(after(keeper, grad_down), (own, came_near, far_came), low, up)
-    grad_up = collect(after(asked, values), got_up_terms, kept, "collect_up")
+    values, grad_up = values_out(
+        after(asked, grad_down), keeper, got_up_terms, kept, (own, came_near, far_came), low, up
+    )
     return values, grad_inputs, grad_down, grad_up
 
 
@@ -492,9 +511,8 @@
     sent_up_terms, low = up_terms(keeper, (low_sum,), dy, count_dp)
     got_up_terms = exchange(sent_up_terms)
     grad_inputs = grad_inputs_out(none, keeper, (full_dy,), w, grad_low, down)
-    values = values_out(keeper, (own,), low, up)
     grad_down = collect(asked, got_terms, kept, "collect_down")
-    grad_up = collect(asked, got_up_terms, kept, "collect_up")
+    values, grad_up = values_out(asked, keeper, got_up_terms, kept, (own,), low, up)
     return values, grad_inputs, grad_down, grad_up
 
 

time: 128 us -> 121 us (0.945)
  waiting for transfers between devices: 37.9 us -> 24.3 us
  blocking collectives: 0 us -> 8.34 us
  starting transfers between devices: 32.3 us -> 30.4 us
    ppermute x10, waiting for transfers between devices: 34.6 us -> 13.3 us  [permute(): return lax.ppermute(a, 'tensor', pairs)]
    all_to_all x0 -> x1, blocking collectives: none -> 8.34 us  [exchange(): return lax.all_to_all(a, 'dp', split_axis=0, concat_axis=0, tiled=True)]
    all_to_all x5 -> x4, waiting for transfers between devices: 3.26 us -> 11 us  [exchange(): return lax.all_to_all(a, 'dp', split_axis=0, concat_axis=0, tiled=True)]
    all_to_all x5 -> x4, starting transfers between devices: 19.8 us -> 15.8 us  [exchange(): return lax.all_to_all(a, 'dp', split_axis=0, concat_axis=0, tiled=True)]
    convert_element_type x1 -> x2, other arithmetic: 0.04 us -> 2.63 us  [on_line(): passed = permute(part.astype(BF), FAR_SWAP)]
    ppermute x10, starting transfers between devices: 12.5 us -> 14.6 us  [permute(): return lax.ppermute(a, 'tensor', pairs)]
    convert_element_type x1 -> x0, other arithmetic: 1.79 us -> none  [on_line(): grad_low_sum = (part, permute(part.astype(BF), FAR_SWAP))]
    pallas_call x2 -> x1, Pallas kernels: 5.54 us -> 3.99 us  [collect(): call(functools.partial(collect_kernel, count_dp, kept), name, array((kept...]
  transfers between devices with their start and end apart: 15 -> 14, of which waited for: 6 -> 8; matrix products, arithmetic and copies ran while one was open for 1% -> 2% of each run, Pallas kernels for 38% -> 39%
where the time goes in v2:
time: 121 us; the launch traced here: 120 us
  Pallas kernels  50.4 us (42%)
  starting transfers between devices  30.4 us (25%)
  waiting for transfers between devices  24.3 us (20%)
  blocking collectives  8.34 us (7%)
  local copies, waits for them, and re-layouts  2.88 us (2%)
  other arithmetic  2.63 us (2%)
    all_to_all x4, starting transfers between devices, exchange(): return lax.all_to_all(a, 'dp', split_axis=0, concat_axis=0, tiled=True)  15.8 us
    ppermute x10, starting transfers between devices, permute(): return lax.ppermute(a, 'tensor', pairs)  14.6 us
    pallas_call x3, Pallas kernels, frozen(): call(functools.partial(frozen_kernel, runs), name, (array((rows, width),...  13.7 us
    ppermute x10, waiting for transfers between devices, permute(): return lax.ppermute(a, 'tensor', pairs)  13.3 us
    all_to_all x4, waiting for transfers between devices, exchange(): return lax.all_to_all(a, 'dp', split_axis=0, concat_axis=0, tiled=True)  11 us
    pallas_call x1, Pallas kernels, grad_inputs_out(): call(functools.partial(grad_inputs_kernel, nblocks, len(pieces)), 'grad_i...  9.42 us
    all_to_all x1, blocking collectives, exchange(): return lax.all_to_all(a, 'dp', split_axis=0, concat_axis=0, tiled=True)  8.34 us
    pallas_call x2, Pallas kernels, select(): call(functools.partial(select_kernel, count_dp), name, array(shape, BF),...  5.47 us
  transfers between devices with their start and end apart: 14, of which 8 were waited for; matrix products, arithmetic and copies ran while one was open for 2% of the time, Pallas kernels for 39%

profile of v2, /device:TPU:0, one launch (start us, length us, event | category | flops | bytes accessed | tf_op | source)
XLA Modules:
  0.0 119.8 jit_solution(13890940346317197964)
XLA Ops:
  0.6 0.0 copy-start
  0.6 3.1 %collective-permute-start.3 = (bf16[1024,256]{1,0:T(8,128)(2,1)}, bf16[1024,256]{1,0:T(8,128)(2,1)S(1)}, u32[]{:S(2)}, u32[]{:S(2)}) collective-permute-start(bf16[1024,256]{1,0:T(8,128)(2,1)} %refs_2_.3), channel_id=1, source_target_pairs={{0,1},{1,0},{2,3},{3,2},{4,5},{5,4},{6,7},{7,6},{8,9},{9,8},{10,11... | collective-permute-start | bytes 1572872 | tf_op jit(solution)/shard_map/ppermute | solution.py:446
  3.7 2.6 %collective-permute-start.2 = (bf16[1024,256]{1,0:T(8,128)(2,1)}, bf16[1024,256]{1,0:T(8,128)(2,1)S(1)}, u32[]{:S(2)}, u32[]{:S(2)}) collective-permute-start(bf16[1024,256]{1,0:T(8,128)(2,1)} %refs_2_.3), channel_id=1, source_target_pairs={{0,2},{2,0},{1,3},{3,1},{4,6},{6,4},{5,7},{7,5},{8,10},{10,8},{9,1... | collective-permute-start | bytes 1572872 | tf_op jit(solution)/shard_map/ppermute | solution.py:446
  6.3 1.3 %request.1 = (s32[8,1,128]{2,1,0:T(1,128)}, s32[8]{0:T(128)}) custom-call(s32[8]{0:T(128)} %per_block_in.1, s32[128]{0:T(128)} %index_in.1), custom_call_target="tpu_custom_call" | custom-call | tf_op jit(solution)/shard_map/request/pallas_call | solution.py:82
  7.6 0.0 copy-start.9
  7.7 8.3 %all_to_all.25.asked = s32[8,1,128]{2,1,0:T(1,128)} all-to-all(s32[8,1,128]{2,1,0:T(1,128)} %get-tuple-element.35), channel_id=1, replica_groups=mesh['dp'=8,'tensor'=4] {'dp'}, dimensions={0} | all-to-all | bytes 8192 | tf_op jit(solution)/shard_map/all_to_all | solution.py:442
  16.0 2.4 %select_up.1 = bf16[8,64,256]{2,1,0:T(8,128)(2,1)} custom-call(s32[8,1,128]{2,1,0:T(1,128)} %all_to_all.25.asked, bf16[16,64,256]{2,1,0:T(8,128)(2,1)} %source.1), custom_call_target="tpu_custom_call" | custom-call | tf_op jit(solution)/shard_map/select_up/pallas_call | solution.py:114
  18.4 3.4 %all-to-all-start.1 = ((bf16[8,64,256]{2,1,0:T(8,128)(2,1)}), bf16[8,64,256]{2,1,0:T(8,128)(2,1)S(1)}, u32[]{:S(2)}, u32[]{:S(2)}) async-start(bf16[8,64,256]{2,1,0:T(8,128)(2,1)} %select_up.1), calls=%async_computation.1 | async-start | bytes 524288 | tf_op jit(solution)/shard_map/all_to_all | solution.py:442
  21.8 3.1 %select_down.1 = bf16[8,64,2048]{2,1,0:T(8,128)(2,1)} custom-call(s32[8,1,128]{2,1,0:T(1,128)} %all_to_all.25.asked, bf16[16,64,2048]{2,1,0:T(8,128)(2,1)} %bitcast.3), custom_call_target="tpu_custom_call" | custom-call | tf_op jit(solution)/shard_map/select_down/pallas_call | solution.py:114
  24.9 3.7 %all-to-all-done.1.up.refs_4_ = bf16[8,64,256]{2,1,0:T(8,128)(2,1)S(1)} async-done(((bf16[8,64,256]{2,1,0:T(8,128)(2,1)}), bf16[8,64,256]{2,1,0:T(8,128)(2,1)S(1)}, u32[]{:S(2)}, u32[]{:S(2)}) %all-to-all-start.1) | async-done | bytes 262176 | tf_op jit(solution)/shard_map/all_to_all | solution.py:442
  28.7 0.0 copy-done
  28.7 0.0 copy-done.9
  28.7 0.8 low_gradient.1
  29.5 0.0 copy-start.4
  29.5 0.7 copy-done.4
  30.2 0.0 collective-permute-done.3.refs_1_
  30.2 0.0 collective-permute-done.2.refs_2_
  30.2 0.0 copy-start.2
  30.2 0.8 copy-done.2
  31.0 3.6 %all-to-all-start.2 = ((bf16[8,64,2048]{2,1,0:T(8,128)(2,1)}), bf16[8,64,2048]{2,1,0:T(8,128)(2,1)S(1)}, u32[]{:S(2)}, u32[]{:S(2)}) async-start(bf16[8,64,2048]{2,1,0:T(8,128)(2,1)} %select_down.1), calls=%async_computation.2 | async-start | bytes 4194304 | tf_op jit(solution)/shard_map/all_to_all | solution.py:442
  34.6 0.5 collective-permute-start
  35.1 0.0 copy-start.5
  35.1 4.1 %frozen_own.1.refs_0_ = bf16[1024,256]{1,0:T(8,128)(2,1)} custom-call(s32[1]{0:T(128)} %bitcast.z, bf16[1024,2048]{1,0:T(8,128)(2,1)} %x.7, bf16[2048,1024]{1,0:T(8,128)(2,1)} %refs_4_.1), custom_call_target="tpu_custom_call" | custom-call | tf_op jit(solution)/shard_map/frozen_own/pallas_call | solution.py:262
  39.2 1.3 %collective-permute-done = bf16[8,64,128]{2,1,0:T(8,128)(2,1)} collective-permute-done((bf16[8,64,128]{2,1,0:T(8,128)(2,1)S(1)}, bf16[8,64,128]{2,1,0:T(8,128)(2,1)}, u32[]{:S(2)}, u32[]{:S(2)}) %collective-permute-start) | collective-permute-done | bytes 131104 | tf_op jit(solution)/shard_map/ppermute | solution.py:446
  40.5 0.0 copy-done.5
  40.5 1.6 %fusion.1 = (bf16[8,64,128]{2,1,0:T(8,128)(2,1)S(1)}, f32[8,64,128]{2,1,0:T(8,128)}) fusion(f32[8,64,128]{2,1,0:T(8,128)S(1)} %copy-done.5, bf16[8,64,128]{2,1,0:T(8,128)(2,1)} %collective-permute-done), kind=kLoop, calls=%fused_computation.3 | loop fusion | flops 196608 | bytes 786432 | tf_op jit(solution)/shard_map/convert_element_type | solution.py:468
  42.2 0.8 collective-permute-start.1
  43.0 5.5 %frozen_first.1 = (bf16[1024,256]{1,0:T(8,128)(2,1)}, bf16[1024,256]{1,0:T(8,128)(2,1)}) custom-call(s32[1]{0:T(128)} %bitcast.z, bf16[1024,2048]{1,0:T(8,128)(2,1)} %x.7, bf16[2048,1024]{1,0:T(8,128)(2,1)} %refs_4_.1, bf16[2048,1024]{1,0:T(8,128)(2,1)} %refs_4_.1), custom_call_target="tpu_custom_call" | custom-call | tf_op jit(solution)/shard_map/frozen_first/pallas_call | solution.py:262
  48.5 0.0 copy-start.10
  48.5 2.3 %collective-permute-done.1.refs_1_ = bf16[8,64,128]{2,1,0:T(8,128)(2,1)S(1)} collective-permute-done((bf16[8,64,128]{2,1,0:T(8,128)(2,1)S(1)}, bf16[8,64,128]{2,1,0:T(8,128)(2,1)S(1)}, u32[]{:S(2)}, u32[]{:S(2)}) %collective-permute-start.1) | collective-permute-done | bytes 131104 | tf_op jit(solution)/shard_map/ppermute | solution.py:446
  50.8 0.0 copy-start.11
  50.8 0.0 collective-permute-start.5
  50.8 0.7 copy-done.11
  51.5 5.3 %down_terms.1 = (bf16[8,64,2048]{2,1,0:T(8,128)(2,1)}, bf16[8,64,128]{2,1,0:T(8,128)(2,1)}) custom-call(s32[8]{0:T(128)} %get-tuple-element.56.keeper, f32[8,64,128]{2,1,0:T(8,128)} %get-tuple-element.69.refs_0_, bf16[8,64,128]{2,1,0:T(8,128)(2,1)} %copy-done.11, bf16[1024,2048]{1,0:T(8,128)(2,1)} %x.7), custom_call_target="tpu_custom_call" | custom-call | tf_op jit(solution)/shard_map/down_terms/pallas_call | solution.py:210
  56.8 4.4 %all-to-all-done.2.down.refs_6_ = bf16[8,64,2048]{2,1,0:T(8,128)(2,1)S(1)} async-done(((bf16[8,64,2048]{2,1,0:T(8,128)(2,1)}), bf16[8,64,2048]{2,1,0:T(8,128)(2,1)S(1)}, u32[]{:S(2)}, u32[]{:S(2)}) %all-to-all-start.2) | async-done | bytes 2097184 | tf_op jit(solution)/shard_map/all_to_all | solution.py:442
  61.2 0.0 copy-done.10
  61.2 5.0 %low_partial.1 = (f32[8,64,128]{2,1,0:T(8,128)S(1)}, bf16[8,64,128]{2,1,0:T(8,128)(2,1)S(1)}) custom-call(s32[8]{0:T(128)S(1)} %copy-done.10, bf16[8,64,2048]{2,1,0:T(8,128)(2,1)S(1)} %all-to-all-done.2.down.refs_6_, bf16[1024,2048]{1,0:T(8,128)(2,1)} %x.7), custom_call_target="tpu_custom_call" | custom-call | tf_op jit(solution)/shard_map/low_partial/pallas_call | solution.py:166
  66.2 0.0 copy-start.6
  66.2 0.7 copy-done.6
  66.9 0.0 collective-permute-done.5.refs_1_
  66.9 4.3 %all-to-all-start.3 = ((bf16[8,64,2048]{2,1,0:T(8,128)(2,1)}), bf16[8,64,2048]{2,1,0:T(8,128)(2,1)}, u32[]{:S(2)}, u32[]{:S(2)}) async-start(bf16[8,64,2048]{2,1,0:T(8,128)(2,1)} %get-tuple-element.60), calls=%async_computation.3 | async-start | bytes 4194304 | tf_op jit(solution)/shard_map/all_to_all | solution.py:442
  71.3 0.5 collective-permute-start.4
  71.8 1.6 %collective-permute-start.6 = (bf16[1024,256]{1,0:T(8,128)(2,1)}, bf16[1024,256]{1,0:T(8,128)(2,1)S(1)}, u32[]{:S(2)}, u32[]{:S(2)}) collective-permute-start(bf16[1024,256]{1,0:T(8,128)(2,1)} %copy-done.2), channel_id=1, source_target_pairs={{0,1},{1,0},{2,3},{3,2},{4,5},{5,4},{6,7},{7,6},{8,9},{9,8},{10,11... | collective-permute-start | bytes 1572872 | tf_op jit(solution)/shard_map/ppermute | solution.py:446
  73.4 4.3 %collective-permute-done.4 = bf16[8,64,128]{2,1,0:T(8,128)(2,1)S(1)} collective-permute-done((bf16[8,64,128]{2,1,0:T(8,128)(2,1)S(1)}, bf16[8,64,128]{2,1,0:T(8,128)(2,1)S(1)}, u32[]{:S(2)}, u32[]{:S(2)}) %collective-permute-start.4) | collective-permute-done | bytes 131104 | tf_op jit(solution)/shard_map/ppermute | solution.py:446
  77.6 1.0 fusion
  78.6 0.5 collective-permute-start.7
  79.2 4.2 %frozen_far.1 = bf16[1024,256]{1,0:T(8,128)(2,1)} custom-call(s32[1]{0:T(128)} %bitcast.z, bf16[1024,2048]{1,0:T(8,128)(2,1)} %x.7, bf16[2048,1024]{1,0:T(8,128)(2,1)} %refs_4_.1, bf16[1024,256]{1,0:T(8,128)(2,1)} %collective-permute-done.5.refs_1_), custom_call_target="tpu_custom_call" | custom-call | tf_op jit(solution)/shard_map/frozen_far/pallas_call | solution.py:262
  83.3 2.5 %collective-permute-start.9 = (bf16[1024,256]{1,0:T(8,128)(2,1)}, bf16[1024,256]{1,0:T(8,128)(2,1)}, u32[]{:S(2)}, u32[]{:S(2)}) collective-permute-start(bf16[1024,256]{1,0:T(8,128)(2,1)} %frozen_far.1), channel_id=1, source_target_pairs={{0,2},{2,0},{1,3},{3,1},{4,6},{6,4},{5,7},{7,5},{8,10},{10,8},{9,1... | collective-permute-start | bytes 1572872 | tf_op jit(solution)/shard_map/ppermute | solution.py:446
  85.8 3.9 %collective-permute-done.7.refs_1_ = bf16[8,64,128]{2,1,0:T(8,128)(2,1)S(1)} collective-permute-done((bf16[8,64,128]{2,1,0:T(8,128)(2,1)S(1)}, bf16[8,64,128]{2,1,0:T(8,128)(2,1)S(1)}, u32[]{:S(2)}, u32[]{:S(2)}) %collective-permute-start.7) | collective-permute-done | bytes 131104 | tf_op jit(solution)/shard_map/ppermute | solution.py:446
  89.7 2.5 %collective-permute-start.8 = (bf16[1024,256]{1,0:T(8,128)(2,1)}, bf16[1024,256]{1,0:T(8,128)(2,1)}, u32[]{:S(2)}, u32[]{:S(2)}) collective-permute-start(bf16[1024,256]{1,0:T(8,128)(2,1)} %get-tuple-element.62), channel_id=1, source_target_pairs={{0,1},{1,0},{2,3},{3,2},{4,5},{5,4},{6,7},{7,6},{8,9},{9,8},{10,11... | collective-permute-start | bytes 1572872 | tf_op jit(solution)/shard_map/ppermute | solution.py:446
  92.2 1.4 %collective-permute-done.6.refs_3_ = bf16[1024,256]{1,0:T(8,128)(2,1)S(1)} collective-permute-done((bf16[1024,256]{1,0:T(8,128)(2,1)}, bf16[1024,256]{1,0:T(8,128)(2,1)S(1)}, u32[]{:S(2)}, u32[]{:S(2)}) %collective-permute-start.6) | collective-permute-done | bytes 524320 | tf_op jit(solution)/shard_map/ppermute | solution.py:446
  93.6 0.0 copy-done.3
  93.6 0.0 copy-done.7
  93.6 9.4 %grad_inputs.1 = bf16[1024,2048]{1,0:T(8,128)(2,1)} custom-call(s32[1]{0:T(128)} %bitcast.z, s32[8]{0:T(128)S(1)} %copy-done.10, bf16[1024,256]{1,0:T(8,128)(2,1)S(1)} %copy-done, bf16[1024,256]{1,0:T(8,128)(2,1)S(1)} %collective-permute-done.3.refs_1_, bf16[1024,256]{1,0:T(8,128)(2,1)S(1)} %copy-done.3, ...), custom_call_target="tpu_custom_call" | custom-call | tf_op jit(solution)/shard_map/grad_inputs/pallas_call | solution.py:302
  103.0 1.5 %up_terms.1 = (bf16[8,64,256]{2,1,0:T(8,128)(2,1)}, bf16[8,64,128]{2,1,0:T(8,128)(2,1)S(1)}) custom-call(s32[8]{0:T(128)S(1)} %copy-done.10, f32[8,64,128]{2,1,0:T(8,128)S(1)} %get-tuple-element.67.refs_0_, bf16[8,64,128]{2,1,0:T(8,128)(2,1)S(1)} %collective-permute-done.7.refs_1_, bf16[1024,256]{1,0:T(8,128)(2,1)S(1)} %copy-done), custom_call_target="tpu_custom_call" | custom-call | tf_op jit(solution)/shard_map/up_terms/pallas_call | solution.py:239
  104.5 0.0 all-to-all-done.3.terms
  104.5 4.5 %all-to-all-start.4 = ((bf16[8,64,256]{2,1,0:T(8,128)(2,1)}), bf16[8,64,256]{2,1,0:T(8,128)(2,1)S(1)}, u32[]{:S(2)}, u32[]{:S(2)}) async-start(bf16[8,64,256]{2,1,0:T(8,128)(2,1)} %get-tuple-element.57), calls=%async_computation.4 | async-start | bytes 524288 | tf_op jit(solution)/shard_map/all_to_all | solution.py:442
  109.0 0.0 copy-done.8
  109.0 4.0 %collect_down.1 = bf16[16,64,2048]{2,1,0:T(8,128)(2,1)} custom-call(s32[8,1,128]{2,1,0:T(1,128)S(1)} %copy-done.8, bf16[8,64,2048]{2,1,0:T(8,128)(2,1)} %all-to-all-done.3.terms), custom_call_target="tpu_custom_call" | custom-call | tf_op jit(solution)/shard_map/collect_down/pallas_call | solution.py:405
  113.0 0.0 collective-permute-done.9.refs_2_
  113.0 2.9 %all-to-all-done.4.terms = bf16[8,64,256]{2,1,0:T(8,128)(2,1)S(1)} async-done(((bf16[8,64,256]{2,1,0:T(8,128)(2,1)}), bf16[8,64,256]{2,1,0:T(8,128)(2,1)S(1)}, u32[]{:S(2)}, u32[]{:S(2)}) %all-to-all-start.4) | async-done | bytes 262176 | tf_op jit(solution)/shard_map/all_to_all | solution.py:442
  115.9 0.0 collective-permute-done.8.refs_1_
  115.9 0.0 copy-done.1
  115.9 3.9 %values.1 = (bf16[1024,256]{1,0:T(8,128)(2,1)}, bf16[16,64,256]{2,1,0:T(8,128)(2,1)}) custom-call(s32[8,1,128]{2,1,0:T(1,128)S(1)} %copy-done.8, s32[8]{0:T(128)S(1)} %copy-done.10, bf16[8,64,256]{2,1,0:T(8,128)(2,1)S(1)} %all-to-all-done.4.terms, bf16[1024,256]{1,0:T(8,128)(2,1)S(1)} %copy-done.1, bf16[1024,256]{1,0:T(8,128)(2,1)} %collective-permute-done.8.refs_1_, ...), custom_call_target="tpu_custom_call" | custom-call | tf_op jit(solution)/shard_map/values/pallas_call | solution.py:431
  (4 shorter events, 0.0 us)
Async XLA Ops:
  0.6 28.0 %copy-start = (bf16[1024,256]{1,0:T(8,128)(2,1)S(1)}, bf16[1024,256]{1,0:T(8,128)(2,1)}, u32[]{:S(2)}) copy-start(bf16[1024,256]{1,0:T(8,128)(2,1)} %refs_2_.3) | copy-start | bytes 1572868
  0.6 29.6 %collective-permute-start.3 = (bf16[1024,256]{1,0:T(8,128)(2,1)}, bf16[1024,256]{1,0:T(8,128)(2,1)S(1)}, u32[]{:S(2)}, u32[]{:S(2)}) collective-permute-start(bf16[1024,256]{1,0:T(8,128)(2,1)} %refs_2_.3), channel_id=1, source_target_pairs={{0,1},{1,0},{2,3},{3,2},{4,5},{5,4},{6,7},{7,6},{8,9},{9,8},{10,11... | collective-permute-start | bytes 1572872 | tf_op jit(solution)/shard_map/ppermute | solution.py:446
  3.7 26.5 %collective-permute-start.2 = (bf16[1024,256]{1,0:T(8,128)(2,1)}, bf16[1024,256]{1,0:T(8,128)(2,1)S(1)}, u32[]{:S(2)}, u32[]{:S(2)}) collective-permute-start(bf16[1024,256]{1,0:T(8,128)(2,1)} %refs_2_.3), channel_id=1, source_target_pairs={{0,2},{2,0},{1,3},{3,1},{4,6},{6,4},{5,7},{7,5},{8,10},{10,8},{9,1... | collective-permute-start | bytes 1572872 | tf_op jit(solution)/shard_map/ppermute | solution.py:446
  7.6 21.0 %copy-start.9 = (s32[8]{0:T(128)S(1)}, s32[8]{0:T(128)}, u32[]{:S(2)}) copy-start(s32[8]{0:T(128)} %get-tuple-element.56.keeper) | copy-start | bytes 100
  18.4 10.3 %all-to-all-start.1 = ((bf16[8,64,256]{2,1,0:T(8,128)(2,1)}), bf16[8,64,256]{2,1,0:T(8,128)(2,1)S(1)}, u32[]{:S(2)}, u32[]{:S(2)}) async-start(bf16[8,64,256]{2,1,0:T(8,128)(2,1)} %select_up.1), calls=%async_computation.1 | async-start | bytes 524288 | tf_op jit(solution)/shard_map/all_to_all | solution.py:442
  29.5 0.7 copy-start.4
  30.2 0.8 copy-start.2
  31.0 30.2 %all-to-all-start.2 = ((bf16[8,64,2048]{2,1,0:T(8,128)(2,1)}), bf16[8,64,2048]{2,1,0:T(8,128)(2,1)S(1)}, u32[]{:S(2)}, u32[]{:S(2)}) async-start(bf16[8,64,2048]{2,1,0:T(8,128)(2,1)} %select_down.1), calls=%async_computation.2 | async-start | bytes 4194304 | tf_op jit(solution)/shard_map/all_to_all | solution.py:442
  34.6 5.9 %collective-permute-start = (bf16[8,64,128]{2,1,0:T(8,128)(2,1)S(1)}, bf16[8,64,128]{2,1,0:T(8,128)(2,1)}, u32[]{:S(2)}, u32[]{:S(2)}) collective-permute-start(bf16[8,64,128]{2,1,0:T(8,128)(2,1)S(1)} %get-tuple-element.42), channel_id=1, source_target_pairs={{0,1},{1,0},{2,3},{3,2},{4,5},{5,4},{6,7},{7,6},{8,9},{9,8},{10,11... | collective-permute-start | bytes 393224 | tf_op jit(solution)/shard_map/ppermute | solution.py:446
  35.1 5.4 %copy-start.5 = (f32[8,64,128]{2,1,0:T(8,128)S(1)}, f32[8,64,128]{2,1,0:T(8,128)}, u32[]{:S(2)}) copy-start(f32[8,64,128]{2,1,0:T(8,128)} %copy-done.4) | copy-start | bytes 786436
  42.2 8.6 %collective-permute-start.1 = (bf16[8,64,128]{2,1,0:T(8,128)(2,1)S(1)}, bf16[8,64,128]{2,1,0:T(8,128)(2,1)S(1)}, u32[]{:S(2)}, u32[]{:S(2)}) collective-permute-start(bf16[8,64,128]{2,1,0:T(8,128)(2,1)S(1)} %get-tuple-element.68), channel_id=1, source_target_pairs={{0,2},{2,0},{1,3},{3,1},{4,6},{6,4},{5,7},{7,5},{8,10},{10,8},{9,1... | collective-permute-start | bytes 393224 | tf_op jit(solution)/shard_map/ppermute | solution.py:446
  48.5 12.7 %copy-start.10 = (s32[8]{0:T(128)S(1)}, s32[8]{0:T(128)}, u32[]{:S(2)}) copy-start(s32[8]{0:T(128)} %get-tuple-element.56.keeper) | copy-start | bytes 100
  50.8 0.7 copy-start.11
  50.8 16.1 %collective-permute-start.5 = (bf16[1024,256]{1,0:T(8,128)(2,1)}, bf16[1024,256]{1,0:T(8,128)(2,1)}, u32[]{:S(2)}, u32[]{:S(2)}) collective-permute-start(bf16[1024,256]{1,0:T(8,128)(2,1)} %get-tuple-element.53), channel_id=1, source_target_pairs={{0,1},{1,0},{2,3},{3,2},{4,5},{5,4},{6,7},{7,6},{8,9},{9,8},{10,11... | collective-permute-start | bytes 1572872 | tf_op jit(solution)/shard_map/ppermute | solution.py:446
  66.2 0.7 copy-start.6
  66.9 37.6 %all-to-all-start.3 = ((bf16[8,64,2048]{2,1,0:T(8,128)(2,1)}), bf16[8,64,2048]{2,1,0:T(8,128)(2,1)}, u32[]{:S(2)}, u32[]{:S(2)}) async-start(bf16[8,64,2048]{2,1,0:T(8,128)(2,1)} %get-tuple-element.60), calls=%async_computation.3 | async-start | bytes 4194304 | tf_op jit(solution)/shard_map/all_to_all | solution.py:442
  71.3 6.4 %collective-permute-start.4 = (bf16[8,64,128]{2,1,0:T(8,128)(2,1)S(1)}, bf16[8,64,128]{2,1,0:T(8,128)(2,1)S(1)}, u32[]{:S(2)}, u32[]{:S(2)}) collective-permute-start(bf16[8,64,128]{2,1,0:T(8,128)(2,1)S(1)} %get-tuple-element.50), channel_id=1, source_target_pairs={{0,1},{1,0},{2,3},{3,2},{4,5},{5,4},{6,7},{7,6},{8,9},{9,8},{10,11... | collective-permute-start | bytes 393224 | tf_op jit(solution)/shard_map/ppermute | solution.py:446
  71.8 21.8 %collective-permute-start.6 = (bf16[1024,256]{1,0:T(8,128)(2,1)}, bf16[1024,256]{1,0:T(8,128)(2,1)S(1)}, u32[]{:S(2)}, u32[]{:S(2)}) collective-permute-start(bf16[1024,256]{1,0:T(8,128)(2,1)} %copy-done.2), channel_id=1, source_target_pairs={{0,1},{1,0},{2,3},{3,2},{4,5},{5,4},{6,7},{7,6},{8,9},{9,8},{10,11... | collective-permute-start | bytes 1572872 | tf_op jit(solution)/shard_map/ppermute | solution.py:446
  78.6 11.1 %collective-permute-start.7 = (bf16[8,64,128]{2,1,0:T(8,128)(2,1)S(1)}, bf16[8,64,128]{2,1,0:T(8,128)(2,1)S(1)}, u32[]{:S(2)}, u32[]{:S(2)}) collective-permute-start(bf16[8,64,128]{2,1,0:T(8,128)(2,1)S(1)} %get-tuple-element.66), channel_id=1, source_target_pairs={{0,2},{2,0},{1,3},{3,1},{4,6},{6,4},{5,7},{7,5},{8,10},{10,8},{9,1... | collective-permute-start | bytes 393224 | tf_op jit(solution)/shard_map/ppermute | solution.py:446
  79.1 14.5 %copy-start.3 = (bf16[1024,256]{1,0:T(8,128)(2,1)S(1)}, bf16[1024,256]{1,0:T(8,128)(2,1)}, u32[]{:S(2)}) copy-start(bf16[1024,256]{1,0:T(8,128)(2,1)} %copy-done.2) | copy-start | bytes 1572868
  79.1 14.5 %copy-start.7 = (bf16[8,64,128]{2,1,0:T(8,128)(2,1)S(1)}, bf16[8,64,128]{2,1,0:T(8,128)(2,1)}, u32[]{:S(2)}) copy-start(bf16[8,64,128]{2,1,0:T(8,128)(2,1)} %get-tuple-element.46.refs_5_) | copy-start | bytes 393220
  83.3 25.6 %copy-start.8 = (s32[8,1,128]{2,1,0:T(1,128)S(1)}, s32[8,1,128]{2,1,0:T(1,128)}, u32[]{:S(2)}) copy-start(s32[8,1,128]{2,1,0:T(1,128)} %all_to_all.25.asked) | copy-start | bytes 12292
  83.3 29.6 %collective-permute-start.9 = (bf16[1024,256]{1,0:T(8,128)(2,1)}, bf16[1024,256]{1,0:T(8,128)(2,1)}, u32[]{:S(2)}, u32[]{:S(2)}) collective-permute-start(bf16[1024,256]{1,0:T(8,128)(2,1)} %frozen_far.1), channel_id=1, source_target_pairs={{0,2},{2,0},{1,3},{3,1},{4,6},{6,4},{5,7},{7,5},{8,10},{10,8},{9,1... | collective-permute-start | bytes 1572872 | tf_op jit(solution)/shard_map/ppermute | solution.py:446
  89.7 26.2 %collective-permute-start.8 = (bf16[1024,256]{1,0:T(8,128)(2,1)}, bf16[1024,256]{1,0:T(8,128)(2,1)}, u32[]{:S(2)}, u32[]{:S(2)}) collective-permute-start(bf16[1024,256]{1,0:T(8,128)(2,1)} %get-tuple-element.62), channel_id=1, source_target_pairs={{0,1},{1,0},{2,3},{3,2},{4,5},{5,4},{6,7},{7,6},{8,9},{9,8},{10,11... | collective-permute-start | bytes 1572872 | tf_op jit(solution)/shard_map/ppermute | solution.py:446
  103.0 12.9 %copy-start.1 = (bf16[1024,256]{1,0:T(8,128)(2,1)S(1)}, bf16[1024,256]{1,0:T(8,128)(2,1)}, u32[]{:S(2)}) copy-start(bf16[1024,256]{1,0:T(8,128)(2,1)} %frozen_own.1.refs_0_) | copy-start | bytes 1572868
  104.5 11.4 %all-to-all-start.4 = ((bf16[8,64,256]{2,1,0:T(8,128)(2,1)}), bf16[8,64,256]{2,1,0:T(8,128)(2,1)S(1)}, u32[]{:S(2)}, u32[]{:S(2)}) async-start(bf16[8,64,256]{2,1,0:T(8,128)(2,1)} %get-tuple-element.57), calls=%async_computation.4 | async-start | bytes 524288 | tf_op jit(solution)/shard_map/all_to_all | solution.py:442

commit v3 on v2

--- a/solution.py
+++ b/solution.py
@@ -13,6 +13,8 @@
 F32 = jnp.float32
 VMEM_LIMIT = 48 * 1024 * 1024
 ALL_VMEM = 57 * 1024 * 1024
+LESS_VMEM = 24 * 1024 * 1024
+SMALLER = ("frozen_far",)
 LANES = 128
 
 SWAP = [(0, 1), (1, 0), (2, 3), (3, 2)]
@@ -263,7 +265,7 @@
         functools.partial(frozen_kernel, runs),
         name,
         (array((rows, width), dtype),) * runs,
-        limit=ALL_VMEM,
+        limit=LESS_VMEM if name in SMALLER else ALL_VMEM,
         grid_spec=pltpu.PrefetchScalarGridSpec(
             num_scalar_prefetch=1,
             grid=(rows // tile,),

time: 121 us -> 120 us (level)
  waiting for transfers between devices: 24.3 us -> 19.6 us
  local copies, waits for them, and re-layouts: 2.88 us -> 7.24 us
    unnamed x24 -> x28, local copies, waits for them, and re-layouts: 2.88 us -> 7.24 us
    all_to_all x4, waiting for transfers between devices: 11 us -> 7.89 us  [exchange(): return lax.all_to_all(a, 'dp', split_axis=0, concat_axis=0, tiled=True)]
    ppermute x10, waiting for transfers between devices: 13.3 us -> 11.7 us  [permute(): return lax.ppermute(a, 'tensor', pairs)]
  transfers between devices with their start and end apart: 14 -> 14, of which waited for: 8 -> 9; matrix products, arithmetic and copies ran while one was open for 2% -> 2% of each run, Pallas kernels for 39% -> 39%
where the time goes in v3:
time: 120 us; the launch traced here: 119 us
  Pallas kernels  50.6 us (42%)
  starting transfers between devices  30.1 us (25%)
  waiting for transfers between devices  19.6 us (16%)
  blocking collectives  8.29 us (7%)
  local copies, waits for them, and re-layouts  7.24 us (6%)
  other arithmetic  2.64 us (2%)
    all_to_all x4, starting transfers between devices, exchange(): return lax.all_to_all(a, 'dp', split_axis=0, concat_axis=0, tiled=True)  15.4 us
    ppermute x10, starting transfers between devices, permute(): return lax.ppermute(a, 'tensor', pairs)  14.7 us
    pallas_call x3, Pallas kernels, frozen(): call(functools.partial(frozen_kernel, runs), name, (array((rows, width),...  12.7 us
    ppermute x10, waiting for transfers between devices, permute(): return lax.ppermute(a, 'tensor', pairs)  11.7 us
    pallas_call x1, Pallas kernels, grad_inputs_out(): call(functools.partial(grad_inputs_kernel, nblocks, len(pieces)), 'grad_i...  9.42 us
    all_to_all x1, blocking collectives, exchange(): return lax.all_to_all(a, 'dp', split_axis=0, concat_axis=0, tiled=True)  8.29 us
    all_to_all x4, waiting for transfers between devices, exchange(): return lax.all_to_all(a, 'dp', split_axis=0, concat_axis=0, tiled=True)  7.89 us
    unnamed x28, local copies, waits for them, and re-layouts  7.24 us
  transfers between devices with their start and end apart: 14, of which 9 were waited for; matrix products, arithmetic and copies ran while one was open for 2% of the time, Pallas kernels for 39%

profile of v3, /device:TPU:0, one launch (start us, length us, event | category | flops | bytes accessed | tf_op | source)
XLA Modules:
  0.0 119.3 jit_solution(11791538937719953487)
XLA Ops:
  0.6 0.0 copy-start.2
  0.6 3.1 %collective-permute-start.3 = (bf16[1024,256]{1,0:T(8,128)(2,1)}, bf16[1024,256]{1,0:T(8,128)(2,1)S(1)}, u32[]{:S(2)}, u32[]{:S(2)}) collective-permute-start(bf16[1024,256]{1,0:T(8,128)(2,1)} %refs_2_.3), channel_id=1, source_target_pairs={{0,1},{1,0},{2,3},{3,2},{4,5},{5,4},{6,7},{7,6},{8,9},{9,8},{10,11... | collective-permute-start | bytes 1572872 | tf_op jit(solution)/shard_map/ppermute | solution.py:448
  3.7 2.6 %collective-permute-start.2 = (bf16[1024,256]{1,0:T(8,128)(2,1)}, bf16[1024,256]{1,0:T(8,128)(2,1)S(1)}, u32[]{:S(2)}, u32[]{:S(2)}) collective-permute-start(bf16[1024,256]{1,0:T(8,128)(2,1)} %refs_2_.3), channel_id=1, source_target_pairs={{0,2},{2,0},{1,3},{3,1},{4,6},{6,4},{5,7},{7,5},{8,10},{10,8},{9,1... | collective-permute-start | bytes 1572872 | tf_op jit(solution)/shard_map/ppermute | solution.py:448
  6.3 1.3 %request.1 = (s32[8,1,128]{2,1,0:T(1,128)}, s32[8]{0:T(128)}) custom-call(s32[8]{0:T(128)} %per_block_in.1, s32[128]{0:T(128)} %index_in.1), custom_call_target="tpu_custom_call" | custom-call | tf_op jit(solution)/shard_map/request/pallas_call | solution.py:84
  7.6 0.0 copy-start.11
  7.7 8.3 %all_to_all.25.asked = s32[8,1,128]{2,1,0:T(1,128)} all-to-all(s32[8,1,128]{2,1,0:T(1,128)} %get-tuple-element.35), channel_id=1, replica_groups=mesh['dp'=8,'tensor'=4] {'dp'}, dimensions={0} | all-to-all | bytes 8192 | tf_op jit(solution)/shard_map/all_to_all | solution.py:444
  16.0 2.4 %select_up.1 = bf16[8,64,256]{2,1,0:T(8,128)(2,1)} custom-call(s32[8,1,128]{2,1,0:T(1,128)} %all_to_all.25.asked, bf16[16,64,256]{2,1,0:T(8,128)(2,1)} %source.1), custom_call_target="tpu_custom_call" | custom-call | tf_op jit(solution)/shard_map/select_up/pallas_call | solution.py:116
  18.3 3.4 %all-to-all-start.1 = ((bf16[8,64,256]{2,1,0:T(8,128)(2,1)}), bf16[8,64,256]{2,1,0:T(8,128)(2,1)S(1)}, u32[]{:S(2)}, u32[]{:S(2)}) async-start(bf16[8,64,256]{2,1,0:T(8,128)(2,1)} %select_up.1), calls=%async_computation.1 | async-start | bytes 524288 | tf_op jit(solution)/shard_map/all_to_all | solution.py:444
  21.7 3.5 %select_down.1 = bf16[8,64,2048]{2,1,0:T(8,128)(2,1)} custom-call(s32[8,1,128]{2,1,0:T(1,128)} %all_to_all.25.asked, bf16[16,64,2048]{2,1,0:T(8,128)(2,1)} %bitcast.3), custom_call_target="tpu_custom_call" | custom-call | tf_op jit(solution)/shard_map/select_down/pallas_call | solution.py:116
  25.2 3.4 %all-to-all-done.1.up.refs_4_ = bf16[8,64,256]{2,1,0:T(8,128)(2,1)S(1)} async-done(((bf16[8,64,256]{2,1,0:T(8,128)(2,1)}), bf16[8,64,256]{2,1,0:T(8,128)(2,1)S(1)}, u32[]{:S(2)}, u32[]{:S(2)}) %all-to-all-start.1) | async-done | bytes 262176 | tf_op jit(solution)/shard_map/all_to_all | solution.py:444
  28.6 0.0 copy-done.2
  28.6 0.0 copy-done.11
  28.6 0.8 low_gradient.1
  29.5 0.0 copy-start.6
  29.5 0.7 copy-done.6
  30.2 0.0 collective-permute-done.3.refs_1_
  30.2 0.0 collective-permute-done.2.refs_2_
  30.2 0.0 copy-start.4
  30.2 0.8 copy-done.4
  31.0 3.6 %all-to-all-start.2 = ((bf16[8,64,2048]{2,1,0:T(8,128)(2,1)}), bf16[8,64,2048]{2,1,0:T(8,128)(2,1)S(1)}, u32[]{:S(2)}, u32[]{:S(2)}) async-start(bf16[8,64,2048]{2,1,0:T(8,128)(2,1)} %select_down.1), calls=%async_computation.2 | async-start | bytes 4194304 | tf_op jit(solution)/shard_map/all_to_all | solution.py:444
  34.6 0.5 collective-permute-start
  35.1 0.0 copy-start.7
  35.1 4.0 %frozen_own.1.refs_0_ = bf16[1024,256]{1,0:T(8,128)(2,1)} custom-call(s32[1]{0:T(128)} %bitcast.z, bf16[1024,2048]{1,0:T(8,128)(2,1)} %x.7, bf16[2048,1024]{1,0:T(8,128)(2,1)} %refs_4_.1), custom_call_target="tpu_custom_call" | custom-call | tf_op jit(solution)/shard_map/frozen_own/pallas_call | solution.py:264
  39.2 1.3 %collective-permute-done = bf16[8,64,128]{2,1,0:T(8,128)(2,1)} collective-permute-done((bf16[8,64,128]{2,1,0:T(8,128)(2,1)S(1)}, bf16[8,64,128]{2,1,0:T(8,128)(2,1)}, u32[]{:S(2)}, u32[]{:S(2)}) %collective-permute-start) | collective-permute-done | bytes 131104 | tf_op jit(solution)/shard_map/ppermute | solution.py:448
  40.5 0.0 copy-done.7
  40.5 1.6 %fusion.1 = (bf16[8,64,128]{2,1,0:T(8,128)(2,1)S(1)}, f32[8,64,128]{2,1,0:T(8,128)}) fusion(f32[8,64,128]{2,1,0:T(8,128)S(1)} %copy-done.7, bf16[8,64,128]{2,1,0:T(8,128)(2,1)} %collective-permute-done), kind=kLoop, calls=%fused_computation.3 | loop fusion | flops 196608 | bytes 786432 | tf_op jit(solution)/shard_map/convert_element_type | solution.py:470
  42.1 0.8 collective-permute-start.1
  43.0 5.5 %frozen_first.1 = (bf16[1024,256]{1,0:T(8,128)(2,1)}, bf16[1024,256]{1,0:T(8,128)(2,1)}) custom-call(s32[1]{0:T(128)} %bitcast.z, bf16[1024,2048]{1,0:T(8,128)(2,1)} %x.7, bf16[2048,1024]{1,0:T(8,128)(2,1)} %refs_4_.1, bf16[2048,1024]{1,0:T(8,128)(2,1)} %refs_4_.1), custom_call_target="tpu_custom_call" | custom-call | tf_op jit(solution)/shard_map/frozen_first/pallas_call | solution.py:264
  48.5 2.3 %collective-permute-done.1.refs_1_ = bf16[8,64,128]{2,1,0:T(8,128)(2,1)S(1)} collective-permute-done((bf16[8,64,128]{2,1,0:T(8,128)(2,1)S(1)}, bf16[8,64,128]{2,1,0:T(8,128)(2,1)S(1)}, u32[]{:S(2)}, u32[]{:S(2)}) %collective-permute-start.1) | collective-permute-done | bytes 131104 | tf_op jit(solution)/shard_map/ppermute | solution.py:448
  50.8 0.0 collective-permute-start.5
  50.8 0.7 copy-done.13
  51.4 5.3 %down_terms.1 = (bf16[8,64,2048]{2,1,0:T(8,128)(2,1)}, bf16[8,64,128]{2,1,0:T(8,128)(2,1)}) custom-call(s32[8]{0:T(128)} %get-tuple-element.56.keeper, f32[8,64,128]{2,1,0:T(8,128)} %get-tuple-element.69.refs_0_, bf16[8,64,128]{2,1,0:T(8,128)(2,1)} %copy-done.13, bf16[1024,2048]{1,0:T(8,128)(2,1)} %x.7), custom_call_target="tpu_custom_call" | custom-call | tf_op jit(solution)/shard_map/down_terms/pallas_call | solution.py:212
  56.8 4.4 %all-to-all-done.2.down.refs_6_ = bf16[8,64,2048]{2,1,0:T(8,128)(2,1)S(1)} async-done(((bf16[8,64,2048]{2,1,0:T(8,128)(2,1)}), bf16[8,64,2048]{2,1,0:T(8,128)(2,1)S(1)}, u32[]{:S(2)}, u32[]{:S(2)}) %all-to-all-start.2) | async-done | bytes 2097184 | tf_op jit(solution)/shard_map/all_to_all | solution.py:444
  61.2 0.0 copy-done.12
  61.2 5.0 %low_partial.1 = (f32[8,64,128]{2,1,0:T(8,128)S(1)}, bf16[8,64,128]{2,1,0:T(8,128)(2,1)S(1)}) custom-call(s32[8]{0:T(128)S(1)} %copy-done.12, bf16[8,64,2048]{2,1,0:T(8,128)(2,1)S(1)} %all-to-all-done.2.down.refs_6_, bf16[1024,2048]{1,0:T(8,128)(2,1)} %x.7), custom_call_target="tpu_custom_call" | custom-call | tf_op jit(solution)/shard_map/low_partial/pallas_call | solution.py:168
  66.1 0.0 copy-start.8
  66.2 0.7 copy-done.8
  66.9 0.0 collective-permute-done.5.refs_1_
  66.9 4.3 %all-to-all-start.3 = ((bf16[8,64,2048]{2,1,0:T(8,128)(2,1)}), bf16[8,64,2048]{2,1,0:T(8,128)(2,1)}, u32[]{:S(2)}, u32[]{:S(2)}) async-start(bf16[8,64,2048]{2,1,0:T(8,128)(2,1)} %get-tuple-element.60), calls=%async_computation.3 | async-start | bytes 4194304 | tf_op jit(solution)/shard_map/all_to_all | solution.py:444
  71.2 0.5 collective-permute-start.4
  71.7 1.6 %collective-permute-start.6 = (bf16[1024,256]{1,0:T(8,128)(2,1)}, bf16[1024,256]{1,0:T(8,128)(2,1)S(1)}, u32[]{:S(2)}, u32[]{:S(2)}) collective-permute-start(bf16[1024,256]{1,0:T(8,128)(2,1)} %copy-done.4), channel_id=1, source_target_pairs={{0,1},{1,0},{2,3},{3,2},{4,5},{5,4},{6,7},{7,6},{8,9},{9,8},{10,11... | collective-permute-start | bytes 1572872 | tf_op jit(solution)/shard_map/ppermute | solution.py:448
  73.3 4.3 %collective-permute-done.4 = bf16[8,64,128]{2,1,0:T(8,128)(2,1)S(1)} collective-permute-done((bf16[8,64,128]{2,1,0:T(8,128)(2,1)S(1)}, bf16[8,64,128]{2,1,0:T(8,128)(2,1)S(1)}, u32[]{:S(2)}, u32[]{:S(2)}) %collective-permute-start.4) | collective-permute-done | bytes 131104 | tf_op jit(solution)/shard_map/ppermute | solution.py:448
  77.6 1.0 fusion
  78.6 0.6 collective-permute-start.7
  79.2 2.2 %copy-done = bf16[1024,2048]{1,0:T(8,128)(2,1)S(1)} copy-done((bf16[1024,2048]{1,0:T(8,128)(2,1)S(1)}, bf16[1024,2048]{1,0:T(8,128)(2,1)}, u32[]{:S(2)}) %copy-start) | copy-done | bytes 4194328
  81.3 2.2 %copy-done.1 = bf16[2048,1024]{1,0:T(8,128)(2,1)S(1)} copy-done((bf16[2048,1024]{1,0:T(8,128)(2,1)S(1)}, bf16[2048,1024]{1,0:T(8,128)(2,1)}, u32[]{:S(2)}) %copy-start.1) | copy-done | bytes 4194328
  83.5 3.2 %frozen_far.1 = bf16[1024,256]{1,0:T(8,128)(2,1)} custom-call(s32[1]{0:T(128)} %bitcast.z, bf16[1024,2048]{1,0:T(8,128)(2,1)S(1)} %copy-done, bf16[2048,1024]{1,0:T(8,128)(2,1)S(1)} %copy-done.1, bf16[1024,256]{1,0:T(8,128)(2,1)} %collective-permute-done.5.refs_1_), custom_call_target="tpu_custom_call" | custom-call | tf_op jit(solution)/shard_map/frozen_far/pallas_call | solution.py:264
  86.7 2.4 %collective-permute-start.9 = (bf16[1024,256]{1,0:T(8,128)(2,1)}, bf16[1024,256]{1,0:T(8,128)(2,1)}, u32[]{:S(2)}, u32[]{:S(2)}) collective-permute-start(bf16[1024,256]{1,0:T(8,128)(2,1)} %frozen_far.1), channel_id=1, source_target_pairs={{0,2},{2,0},{1,3},{3,1},{4,6},{6,4},{5,7},{7,5},{8,10},{10,8},{9,1... | collective-permute-start | bytes 1572872 | tf_op jit(solution)/shard_map/ppermute | solution.py:448
  89.1 0.5 collective-permute-done.7.refs_1_
  89.7 2.6 %collective-permute-start.8 = (bf16[1024,256]{1,0:T(8,128)(2,1)}, bf16[1024,256]{1,0:T(8,128)(2,1)}, u32[]{:S(2)}, u32[]{:S(2)}) collective-permute-start(bf16[1024,256]{1,0:T(8,128)(2,1)} %get-tuple-element.62), channel_id=1, source_target_pairs={{0,1},{1,0},{2,3},{3,2},{4,5},{5,4},{6,7},{7,6},{8,9},{9,8},{10,11... | collective-permute-start | bytes 1572872 | tf_op jit(solution)/shard_map/ppermute | solution.py:448
  92.2 0.0 collective-permute-done.6.refs_3_
  92.2 0.0 copy-done.5
  92.2 0.0 copy-done.9
  92.2 9.4 %grad_inputs.1 = bf16[1024,2048]{1,0:T(8,128)(2,1)} custom-call(s32[1]{0:T(128)} %bitcast.z, s32[8]{0:T(128)S(1)} %copy-done.12, bf16[1024,256]{1,0:T(8,128)(2,1)S(1)} %copy-done.2, bf16[1024,256]{1,0:T(8,128)(2,1)S(1)} %collective-permute-done.3.refs_1_, bf16[1024,256]{1,0:T(8,128)(2,1)S(1)} %copy-done.5, ...), custom_call_target="tpu_custom_call" | custom-call | tf_op jit(solution)/shard_map/grad_inputs/pallas_call | solution.py:304
  101.7 1.5 %up_terms.1 = (bf16[8,64,256]{2,1,0:T(8,128)(2,1)}, bf16[8,64,128]{2,1,0:T(8,128)(2,1)S(1)}) custom-call(s32[8]{0:T(128)S(1)} %copy-done.12, f32[8,64,128]{2,1,0:T(8,128)S(1)} %get-tuple-element.67.refs_0_, bf16[8,64,128]{2,1,0:T(8,128)(2,1)S(1)} %collective-permute-done.7.refs_1_, bf16[1024,256]{1,0:T(8,128)(2,1)S(1)} %copy-done.2), custom_call_target="tpu_custom_call" | custom-call | tf_op jit(solution)/shard_map/up_terms/pallas_call | solution.py:241
  103.1 0.0 all-to-all-done.3.terms
  103.1 4.1 %all-to-all-start.4 = ((bf16[8,64,256]{2,1,0:T(8,128)(2,1)}), bf16[8,64,256]{2,1,0:T(8,128)(2,1)S(1)}, u32[]{:S(2)}, u32[]{:S(2)}) async-start(bf16[8,64,256]{2,1,0:T(8,128)(2,1)} %get-tuple-element.57), calls=%async_computation.4 | async-start | bytes 524288 | tf_op jit(solution)/shard_map/all_to_all | solution.py:444
  107.2 0.0 copy-done.10
  107.2 4.6 %collect_down.1 = bf16[16,64,2048]{2,1,0:T(8,128)(2,1)} custom-call(s32[8,1,128]{2,1,0:T(1,128)S(1)} %copy-done.10, bf16[8,64,2048]{2,1,0:T(8,128)(2,1)} %all-to-all-done.3.terms), custom_call_target="tpu_custom_call" | custom-call | tf_op jit(solution)/shard_map/collect_down/pallas_call | solution.py:407
  111.8 2.2 %collective-permute-done.9.refs_2_ = bf16[1024,256]{1,0:T(8,128)(2,1)} collective-permute-done((bf16[1024,256]{1,0:T(8,128)(2,1)}, bf16[1024,256]{1,0:T(8,128)(2,1)}, u32[]{:S(2)}, u32[]{:S(2)}) %collective-permute-start.9) | collective-permute-done | bytes 524320 | tf_op jit(solution)/shard_map/ppermute | solution.py:448
  114.0 0.2 all-to-all-done.4.terms
  114.1 1.1 collective-permute-done.8.refs_1_
  115.2 0.0 copy-done.3
  115.2 4.1 %values.1 = (bf16[1024,256]{1,0:T(8,128)(2,1)}, bf16[16,64,256]{2,1,0:T(8,128)(2,1)}) custom-call(s32[8,1,128]{2,1,0:T(1,128)S(1)} %copy-done.10, s32[8]{0:T(128)S(1)} %copy-done.12, bf16[8,64,256]{2,1,0:T(8,128)(2,1)S(1)} %all-to-all-done.4.terms, bf16[1024,256]{1,0:T(8,128)(2,1)S(1)} %copy-done.3, bf16[1024,256]{1,0:T(8,128)(2,1)} %collective-permute-done.8.refs_1_, ...), custom_call_target="tpu_custom_call" | custom-call | tf_op jit(solution)/shard_map/values/pallas_call | solution.py:433
  (8 shorter events, 0.0 us)
Async XLA Ops:
  0.6 28.0 %copy-start.2 = (bf16[1024,256]{1,0:T(8,128)(2,1)S(1)}, bf16[1024,256]{1,0:T(8,128)(2,1)}, u32[]{:S(2)}) copy-start(bf16[1024,256]{1,0:T(8,128)(2,1)} %refs_2_.3) | copy-start | bytes 1572868
  0.6 29.5 %collective-permute-start.3 = (bf16[1024,256]{1,0:T(8,128)(2,1)}, bf16[1024,256]{1,0:T(8,128)(2,1)S(1)}, u32[]{:S(2)}, u32[]{:S(2)}) collective-permute-start(bf16[1024,256]{1,0:T(8,128)(2,1)} %refs_2_.3), channel_id=1, source_target_pairs={{0,1},{1,0},{2,3},{3,2},{4,5},{5,4},{6,7},{7,6},{8,9},{9,8},{10,11... | collective-permute-start | bytes 1572872 | tf_op jit(solution)/shard_map/ppermute | solution.py:448
  3.7 26.4 %collective-permute-start.2 = (bf16[1024,256]{1,0:T(8,128)(2,1)}, bf16[1024,256]{1,0:T(8,128)(2,1)S(1)}, u32[]{:S(2)}, u32[]{:S(2)}) collective-permute-start(bf16[1024,256]{1,0:T(8,128)(2,1)} %refs_2_.3), channel_id=1, source_target_pairs={{0,2},{2,0},{1,3},{3,1},{4,6},{6,4},{5,7},{7,5},{8,10},{10,8},{9,1... | collective-permute-start | bytes 1572872 | tf_op jit(solution)/shard_map/ppermute | solution.py:448
  7.6 21.0 %copy-start.11 = (s32[8]{0:T(128)S(1)}, s32[8]{0:T(128)}, u32[]{:S(2)}) copy-start(s32[8]{0:T(128)} %get-tuple-element.56.keeper) | copy-start | bytes 100
  18.3 10.3 %all-to-all-start.1 = ((bf16[8,64,256]{2,1,0:T(8,128)(2,1)}), bf16[8,64,256]{2,1,0:T(8,128)(2,1)S(1)}, u32[]{:S(2)}, u32[]{:S(2)}) async-start(bf16[8,64,256]{2,1,0:T(8,128)(2,1)} %select_up.1), calls=%async_computation.1 | async-start | bytes 524288 | tf_op jit(solution)/shard_map/all_to_all | solution.py:444
  29.5 0.7 copy-start.6
  30.2 0.8 copy-start.4
  31.0 30.2 %all-to-all-start.2 = ((bf16[8,64,2048]{2,1,0:T(8,128)(2,1)}), bf16[8,64,2048]{2,1,0:T(8,128)(2,1)S(1)}, u32[]{:S(2)}, u32[]{:S(2)}) async-start(bf16[8,64,2048]{2,1,0:T(8,128)(2,1)} %select_down.1), calls=%async_computation.2 | async-start | bytes 4194304 | tf_op jit(solution)/shard_map/all_to_all | solution.py:444
  34.6 5.9 %collective-permute-start = (bf16[8,64,128]{2,1,0:T(8,128)(2,1)S(1)}, bf16[8,64,128]{2,1,0:T(8,128)(2,1)}, u32[]{:S(2)}, u32[]{:S(2)}) collective-permute-start(bf16[8,64,128]{2,1,0:T(8,128)(2,1)S(1)} %get-tuple-element.42), channel_id=1, source_target_pairs={{0,1},{1,0},{2,3},{3,2},{4,5},{5,4},{6,7},{7,6},{8,9},{9,8},{10,11... | collective-permute-start | bytes 393224 | tf_op jit(solution)/shard_map/ppermute | solution.py:448
  35.1 5.4 %copy-start.7 = (f32[8,64,128]{2,1,0:T(8,128)S(1)}, f32[8,64,128]{2,1,0:T(8,128)}, u32[]{:S(2)}) copy-start(f32[8,64,128]{2,1,0:T(8,128)} %copy-done.6) | copy-start | bytes 786436
  42.1 8.6 %collective-permute-start.1 = (bf16[8,64,128]{2,1,0:T(8,128)(2,1)S(1)}, bf16[8,64,128]{2,1,0:T(8,128)(2,1)S(1)}, u32[]{:S(2)}, u32[]{:S(2)}) collective-permute-start(bf16[8,64,128]{2,1,0:T(8,128)(2,1)S(1)} %get-tuple-element.68), channel_id=1, source_target_pairs={{0,2},{2,0},{1,3},{3,1},{4,6},{6,4},{5,7},{7,5},{8,10},{10,8},{9,1... | collective-permute-start | bytes 393224 | tf_op jit(solution)/shard_map/ppermute | solution.py:448
  48.5 12.7 %copy-start.12 = (s32[8]{0:T(128)S(1)}, s32[8]{0:T(128)}, u32[]{:S(2)}) copy-start(s32[8]{0:T(128)} %get-tuple-element.56.keeper) | copy-start | bytes 100
  50.8 0.7 copy-start.13
  50.8 16.1 %collective-permute-start.5 = (bf16[1024,256]{1,0:T(8,128)(2,1)}, bf16[1024,256]{1,0:T(8,128)(2,1)}, u32[]{:S(2)}, u32[]{:S(2)}) collective-permute-start(bf16[1024,256]{1,0:T(8,128)(2,1)} %get-tuple-element.53), channel_id=1, source_target_pairs={{0,1},{1,0},{2,3},{3,2},{4,5},{5,4},{6,7},{7,6},{8,9},{9,8},{10,11... | collective-permute-start | bytes 1572872 | tf_op jit(solution)/shard_map/ppermute | solution.py:448
  66.1 0.7 copy-start.8
  66.9 36.3 %all-to-all-start.3 = ((bf16[8,64,2048]{2,1,0:T(8,128)(2,1)}), bf16[8,64,2048]{2,1,0:T(8,128)(2,1)}, u32[]{:S(2)}, u32[]{:S(2)}) async-start(bf16[8,64,2048]{2,1,0:T(8,128)(2,1)} %get-tuple-element.60), calls=%async_computation.3 | async-start | bytes 4194304 | tf_op jit(solution)/shard_map/all_to_all | solution.py:444
  71.2 6.4 %collective-permute-start.4 = (bf16[8,64,128]{2,1,0:T(8,128)(2,1)S(1)}, bf16[8,64,128]{2,1,0:T(8,128)(2,1)S(1)}, u32[]{:S(2)}, u32[]{:S(2)}) collective-permute-start(bf16[8,64,128]{2,1,0:T(8,128)(2,1)S(1)} %get-tuple-element.50), channel_id=1, source_target_pairs={{0,1},{1,0},{2,3},{3,2},{4,5},{5,4},{6,7},{7,6},{8,9},{9,8},{10,11... | collective-permute-start | bytes 393224 | tf_op jit(solution)/shard_map/ppermute | solution.py:448
  71.7 20.5 %collective-permute-start.6 = (bf16[1024,256]{1,0:T(8,128)(2,1)}, bf16[1024,256]{1,0:T(8,128)(2,1)S(1)}, u32[]{:S(2)}, u32[]{:S(2)}) collective-permute-start(bf16[1024,256]{1,0:T(8,128)(2,1)} %copy-done.4), channel_id=1, source_target_pairs={{0,1},{1,0},{2,3},{3,2},{4,5},{5,4},{6,7},{7,6},{8,9},{9,8},{10,11... | collective-permute-start | bytes 1572872 | tf_op jit(solution)/shard_map/ppermute | solution.py:448
  78.6 11.1 %collective-permute-start.7 = (bf16[8,64,128]{2,1,0:T(8,128)(2,1)S(1)}, bf16[8,64,128]{2,1,0:T(8,128)(2,1)S(1)}, u32[]{:S(2)}, u32[]{:S(2)}) collective-permute-start(bf16[8,64,128]{2,1,0:T(8,128)(2,1)S(1)} %get-tuple-element.66), channel_id=1, source_target_pairs={{0,2},{2,0},{1,3},{3,1},{4,6},{6,4},{5,7},{7,5},{8,10},{10,8},{9,1... | collective-permute-start | bytes 393224 | tf_op jit(solution)/shard_map/ppermute | solution.py:448
  79.2 2.2 %copy-start = (bf16[1024,2048]{1,0:T(8,128)(2,1)S(1)}, bf16[1024,2048]{1,0:T(8,128)(2,1)}, u32[]{:S(2)}) copy-start(bf16[1024,2048]{1,0:T(8,128)(2,1)} %x.7) | copy-start | bytes 12582916
  81.3 2.2 %copy-start.1 = (bf16[2048,1024]{1,0:T(8,128)(2,1)S(1)}, bf16[2048,1024]{1,0:T(8,128)(2,1)}, u32[]{:S(2)}) copy-start(bf16[2048,1024]{1,0:T(8,128)(2,1)} %refs_4_.1) | copy-start | bytes 12582916
  83.5 8.7 %copy-start.5 = (bf16[1024,256]{1,0:T(8,128)(2,1)S(1)}, bf16[1024,256]{1,0:T(8,128)(2,1)}, u32[]{:S(2)}) copy-start(bf16[1024,256]{1,0:T(8,128)(2,1)} %copy-done.4) | copy-start | bytes 1572868
  83.5 8.7 %copy-start.9 = (bf16[8,64,128]{2,1,0:T(8,128)(2,1)S(1)}, bf16[8,64,128]{2,1,0:T(8,128)(2,1)}, u32[]{:S(2)}) copy-start(bf16[8,64,128]{2,1,0:T(8,128)(2,1)} %get-tuple-element.46.refs_5_) | copy-start | bytes 393220
  86.7 20.5 %copy-start.10 = (s32[8,1,128]{2,1,0:T(1,128)S(1)}, s32[8,1,128]{2,1,0:T(1,128)}, u32[]{:S(2)}) copy-start(s32[8,1,128]{2,1,0:T(1,128)} %all_to_all.25.asked) | copy-start | bytes 12292
  86.7 27.3 %collective-permute-start.9 = (bf16[1024,256]{1,0:T(8,128)(2,1)}, bf16[1024,256]{1,0:T(8,128)(2,1)}, u32[]{:S(2)}, u32[]{:S(2)}) collective-permute-start(bf16[1024,256]{1,0:T(8,128)(2,1)} %frozen_far.1), channel_id=1, source_target_pairs={{0,2},{2,0},{1,3},{3,1},{4,6},{6,4},{5,7},{7,5},{8,10},{10,8},{9,1... | collective-permute-start | bytes 1572872 | tf_op jit(solution)/shard_map/ppermute | solution.py:448
  89.7 25.5 %collective-permute-start.8 = (bf16[1024,256]{1,0:T(8,128)(2,1)}, bf16[1024,256]{1,0:T(8,128)(2,1)}, u32[]{:S(2)}, u32[]{:S(2)}) collective-permute-start(bf16[1024,256]{1,0:T(8,128)(2,1)} %get-tuple-element.62), channel_id=1, source_target_pairs={{0,1},{1,0},{2,3},{3,2},{4,5},{5,4},{6,7},{7,6},{8,9},{9,8},{10,11... | collective-permute-start | bytes 1572872 | tf_op jit(solution)/shard_map/ppermute | solution.py:448
  101.7 13.5 %copy-start.3 = (bf16[1024,256]{1,0:T(8,128)(2,1)S(1)}, bf16[1024,256]{1,0:T(8,128)(2,1)}, u32[]{:S(2)}) copy-start(bf16[1024,256]{1,0:T(8,128)(2,1)} %frozen_own.1.refs_0_) | copy-start | bytes 1572868
  103.1 11.0 %all-to-all-start.4 = ((bf16[8,64,256]{2,1,0:T(8,128)(2,1)}), bf16[8,64,256]{2,1,0:T(8,128)(2,1)S(1)}, u32[]{:S(2)}, u32[]{:S(2)}) async-start(bf16[8,64,256]{2,1,0:T(8,128)(2,1)} %get-tuple-element.57), calls=%async_computation.4 | async-start | bytes 524288 | tf_op jit(solution)/shard_map/all_to_all | solution.py:444
